TPU v7x, 32 devices: a whole 2x2x4 slice. The times are simulated.
32 devices in a mesh: ctx: 2 (over x), fsdp: 16 (over z, y, core).
Axes of the slice: x: 2, y: 2, z: 4, core: 2. Of those that a mesh axis runs over, the one named last changes fastest.
Arguments:
- layer_input: bfloat16 [2, 16, 1024, 768], P(None, 'fsdp', 'ctx'), may hold values from -6 to 6
- segments: int32 [2, 16, 1024], P(None, 'fsdp'), may hold values from 0 to 2, as said below
- ln1_gain: bfloat16 [768], P('fsdp'), may hold values from 0.5 to 1.5
- ln1_bias: bfloat16 [768], P('fsdp'), may hold values from -1.1953125 to 1.1953125
- w_qkv: bfloat16 [768, 2304], P('fsdp'), may hold values from -0.21875 to 0.21875
- q_bias: bfloat16 [768], P('fsdp'), may hold values from -1.796875 to 1.796875
- v_bias: bfloat16 [768], P('fsdp'), may hold values from -1.796875 to 1.796875
- w_attn_out: bfloat16 [768, 768], P('fsdp'), may hold values from -0.625 to 0.625
- b_attn_out: bfloat16 [768], P('fsdp'), may hold values from -1.1953125 to 1.1953125
- ln2_gain: bfloat16 [768], P('fsdp'), may hold values from 0.5 to 1.5
- ln2_bias: bfloat16 [768], P('fsdp'), may hold values from -1.1953125 to 1.1953125
- w_up: bfloat16 [768, 3072], P('fsdp'), may hold values from -0.21875 to 0.21875
- b_up: bfloat16 [3072], P('fsdp'), may hold values from -1.1953125 to 1.1953125
- w_down: bfloat16 [3072, 768], P('fsdp'), may hold values from -0.109375 to 0.109375
- b_down: bfloat16 [768], P('fsdp'), may hold values from -1.1953125 to 1.1953125
- cotangent: bfloat16 [2, 16, 1024, 768], P(None, 'fsdp', 'ctx'), may hold values from -6 to 6
Outputs:
- activations: bfloat16 [2, 16, 1024, 768], P(None, 'fsdp', 'ctx')
- input_grad: bfloat16 [2, 16, 1024, 768], P(None, 'fsdp', 'ctx')
- grad_ln1_gain: float32 [768], P('fsdp')
- grad_ln1_bias: float32 [768], P('fsdp')
- grad_w_qkv: float32 [768, 2304], P('fsdp')
- grad_q_bias: float32 [768], P('fsdp')
- grad_v_bias: float32 [768], P('fsdp')
- grad_w_attn_out: float32 [768, 768], P('fsdp')
- grad_b_attn_out: float32 [768], P('fsdp')
- grad_ln2_gain: float32 [768], P('fsdp')
- grad_ln2_bias: float32 [768], P('fsdp')
- grad_w_up: float32 [768, 3072], P('fsdp')
- grad_b_up: float32 [3072], P('fsdp')
- grad_w_down: float32 [3072, 768], P('fsdp')
- grad_b_down: float32 [768], P('fsdp')
Inputs may be any that keep to these rules, and one draw needn't show every extreme that they name: `segments`: along each sequence's positions (stored rows ordered by pos) segment numbers start at 0 and rise by at most one from a position to the next; one document covers exactly the first or exactly the second half of the positions.
All inputs are finite; a program needn't handle non-finite values.
Results may differ from a plain program's by a relative error of at most 0.012.
Values may be sent and summed in bfloat16 or wider, within the bound.
A program may use at most 256 MiB of HBM per device.

v0:
```python
import jax
import jax.numpy as jnp
from jax import lax
from jax.sharding import PartitionSpec as P

H = 12


def stored_positions(length, groups):
    block_size = length // (2 * groups)
    stored = jnp.arange(length, dtype=jnp.int32)
    holder = stored // (2 * block_size)
    within = stored % (2 * block_size)
    second = within // block_size
    offset = within % block_size
    block_index = jnp.where(second == 0, holder, 2 * groups - 1 - holder)
    return block_index * block_size + offset


def normalize_parts(values):
    center = jnp.mean(values, -1, keepdims=True)
    centered = values - center
    inverse = lax.rsqrt(jnp.mean(centered * centered, -1, keepdims=True) + 1e-05)
    return (centered * inverse, inverse)


def normalize_back(grad_normed, normed, inverse):
    first = jnp.mean(grad_normed, -1, keepdims=True)
    second = jnp.mean(grad_normed * normed, -1, keepdims=True)
    return inverse * (grad_normed - first - normed * second)


def tile_allowed(query_pos, query_seg, key_pos, key_seg):
    return (key_pos[None, :] <= query_pos[:, None]) & (key_seg[None, :] == query_seg[:, None])


def tile_scores(query, keys_tile, allowed):
    scores = (
        jnp.einsum("qhd,khd->hqk", query, keys_tile, preferred_element_type=jnp.float32) * 0.125
    )
    return jnp.where(allowed[None], scores, -1e30)


def online_softmax(query, query_pos, query_seg, tiles):
    heads = query.shape[1]
    count_rows = query.shape[0]

    def advance(carry, tile):
        keys_tile, values_tile, key_pos, key_seg = tile
        allowed = tile_allowed(query_pos, query_seg, key_pos, key_seg)

        def compute(state):
            peak, total, accum = state
            scores = tile_scores(query, keys_tile, allowed)
            new_peak = jnp.maximum(peak, jnp.max(scores, -1))
            terms = jnp.where(allowed[None], jnp.exp(scores - new_peak[..., None]), 0.0)
            factor = jnp.exp(peak - new_peak)
            upper = terms.astype(jnp.bfloat16)
            lower = (terms - upper.astype(jnp.float32)).astype(jnp.bfloat16)
            added = jnp.einsum(
                "hqk,khd->qhd", upper, values_tile, preferred_element_type=jnp.float32
            )
            added = added + jnp.einsum(
                "hqk,khd->qhd", lower, values_tile, preferred_element_type=jnp.float32
            )
            accum = accum * jnp.transpose(factor)[..., None] + added
            return (new_peak, total * factor + jnp.sum(terms, -1), accum)

        return (compute(carry), None)

    start_state = (
        jnp.full((heads, count_rows), -1e30, jnp.float32),
        jnp.zeros((heads, count_rows), jnp.float32),
        jnp.zeros(query.shape, jnp.float32),
    )
    (peak, total, accum), unused = lax.scan(advance, start_state, tiles)
    exact = accum / jnp.transpose(total)[..., None]
    return (peak + jnp.log(total), exact)


def attention_out(query, log_total, query_pos, query_seg, tiles):

    def advance(carry, tile):
        keys_tile, values_tile, key_pos, key_seg = tile
        allowed = tile_allowed(query_pos, query_seg, key_pos, key_seg)

        def compute(summed):
            scores = tile_scores(query, keys_tile, allowed)
            probs = jnp.where(allowed[None], jnp.exp(scores - log_total[..., None]), 0.0)
            lowered = probs.astype(jnp.bfloat16)
            return summed + jnp.einsum(
                "hqk,khd->qhd", lowered, values_tile, preferred_element_type=jnp.float32
            )

        return (compute(carry), None)

    summed, unused = lax.scan(advance, jnp.zeros(query.shape, jnp.float32), tiles)
    return summed


def attention_back(query, log_total, grad_attended, delta, query_pos, query_seg, tiles):

    def advance(grad_query, tile):
        keys_tile, values_tile, key_pos, key_seg = tile
        allowed = tile_allowed(query_pos, query_seg, key_pos, key_seg)

        def compute(carry_query):
            scores = tile_scores(query, keys_tile, allowed)
            probs = jnp.where(allowed[None], jnp.exp(scores - log_total[..., None]), 0.0)
            lowered = probs.astype(jnp.bfloat16)
            grad_values = jnp.einsum(
                "hqk,qhd->khd", lowered, grad_attended, preferred_element_type=jnp.float32
            )
            grad_probs = jnp.einsum(
                "qhd,khd->hqk", grad_attended, values_tile, preferred_element_type=jnp.float32
            )
            grad_scores = (probs * (grad_probs - delta[..., None])).astype(jnp.bfloat16)
            new_query = carry_query + 0.125 * jnp.einsum(
                "hqk,khd->qhd", grad_scores, keys_tile, preferred_element_type=jnp.float32
            )
            grad_keys = 0.125 * jnp.einsum(
                "hqk,qhd->khd", grad_scores, query, preferred_element_type=jnp.float32
            )
            return (new_query, grad_keys, grad_values)

        new_query, grad_keys, grad_values = compute(grad_query)
        return (new_query, (grad_keys, grad_values))

    grad_query, (grad_keys, grad_values) = lax.scan(
        advance, jnp.zeros(query.shape, jnp.float32), tiles
    )
    return (grad_query, grad_keys, grad_values)


def column_sums(values):
    return jnp.sum(values.astype(jnp.float32), 0)


def layer_pass(inputs, cots, seg_row, weights, positions, start):
    (
        gain_one,
        shift_one,
        proj_mixed,
        bias_query,
        bias_value,
        proj_out,
        bias_out,
        gain_two,
        shift_two,
        proj_up,
        bias_up,
        proj_down,
        bias_down,
    ) = weights
    count_rows = inputs.shape[0]
    width = inputs.shape[1]
    heads = H
    head_size = width // heads
    length = seg_row.shape[0]
    query_pos = lax.dynamic_slice_in_dim(positions, start, count_rows)
    query_seg = lax.dynamic_slice_in_dim(seg_row, start, count_rows)
    values_in = inputs.astype(jnp.float32)
    normed_one, inverse_one = normalize_parts(values_in)
    lowered_one = (
        normed_one * gain_one.astype(jnp.float32) + shift_one.astype(jnp.float32)
    ).astype(jnp.bfloat16)
    mixed_bias = jnp.concatenate(
        [
            bias_query.astype(jnp.float32),
            jnp.zeros((width,), jnp.float32),
            bias_value.astype(jnp.float32),
        ]
    )
    mixed = (
        jnp.dot(lowered_one, proj_mixed, preferred_element_type=jnp.float32) + mixed_bias
    ).astype(jnp.bfloat16)
    query = mixed[:, :width].reshape(count_rows, heads, head_size)
    keys_values = lax.all_gather(mixed[:, width:], "ctx", axis=0, tiled=True)
    block = min(512, length)
    count = length // block
    tiles = (
        keys_values[:, :width].reshape(count, block, heads, head_size),
        keys_values[:, width:].reshape(count, block, heads, head_size),
        positions.reshape(count, block),
        seg_row.reshape(count, block),
    )
    log_total, exact = online_softmax(query, query_pos, query_seg, tiles)
    summed = attention_out(query, log_total, query_pos, query_seg, tiles)
    attended = summed.reshape(count_rows, width).astype(jnp.bfloat16)
    branch = jnp.dot(attended, proj_out, preferred_element_type=jnp.float32) + bias_out.astype(
        jnp.float32
    )
    resid = values_in + branch
    normed_two, inverse_two = normalize_parts(resid)
    lowered_two = (
        normed_two * gain_two.astype(jnp.float32) + shift_two.astype(jnp.float32)
    ).astype(jnp.bfloat16)
    hidden = jnp.dot(lowered_two, proj_up, preferred_element_type=jnp.float32) + bias_up.astype(
        jnp.float32
    )

    def smooth(pre_active):
        return jax.nn.gelu(pre_active, approximate=True)

    active_full, gelu_back = jax.vjp(smooth, hidden)
    active = active_full.astype(jnp.bfloat16)
    down = jnp.dot(active, proj_down, preferred_element_type=jnp.float32) + bias_down.astype(
        jnp.float32
    )
    output = (resid + down).astype(jnp.bfloat16)
    grad_out = cots.astype(jnp.float32)
    grad_bias_down = column_sums(cots)
    grad_proj_down = jnp.einsum("tf,td->fd", active, cots, preferred_element_type=jnp.float32)
    grad_active = jnp.einsum("td,fd->tf", cots, proj_down, preferred_element_type=jnp.float32)
    grad_hidden = gelu_back(grad_active)[0].astype(jnp.bfloat16)
    grad_bias_up = column_sums(grad_hidden)
    grad_proj_up = jnp.einsum(
        "td,tf->df", lowered_two, grad_hidden, preferred_element_type=jnp.float32
    )
    grad_lowered_two = jnp.einsum(
        "tf,df->td", grad_hidden, proj_up, preferred_element_type=jnp.float32
    )
    grad_gain_two = jnp.sum(grad_lowered_two * normed_two, 0)
    grad_shift_two = jnp.sum(grad_lowered_two, 0)
    grad_resid = grad_out + normalize_back(
        grad_lowered_two * gain_two.astype(jnp.float32), normed_two, inverse_two
    )
    grad_branch = grad_resid.astype(jnp.bfloat16)
    grad_bias_out = column_sums(grad_branch)
    grad_proj_out = jnp.einsum(
        "td,te->de", attended, grad_branch, preferred_element_type=jnp.float32
    )
    grad_attended = jnp.einsum(
        "te,de->td", grad_branch, proj_out, preferred_element_type=jnp.float32
    ).astype(jnp.bfloat16)
    grad_attended = grad_attended.reshape(count_rows, heads, head_size)
    delta = jnp.einsum("qhd,qhd->hq", grad_attended.astype(jnp.float32), exact)
    grad_query, grad_keys, grad_values = attention_back(
        query, log_total, grad_attended, delta, query_pos, query_seg, tiles
    )
    grad_pairs = jnp.concatenate(
        [grad_keys.reshape(length, width), grad_values.reshape(length, width)], 1
    )
    grad_pairs_local = lax.psum_scatter(grad_pairs, "ctx", scatter_dimension=0, tiled=True)
    grad_mixed = jnp.concatenate(
        [grad_query.reshape(count_rows, width), grad_pairs_local], 1
    ).astype(jnp.bfloat16)
    grad_bias_query = column_sums(grad_mixed[:, :width])
    grad_bias_value = column_sums(grad_mixed[:, 2 * width :])
    grad_proj_mixed = jnp.einsum(
        "td,te->de", lowered_one, grad_mixed, preferred_element_type=jnp.float32
    )
    grad_lowered_one = jnp.einsum(
        "te,de->td", grad_mixed, proj_mixed, preferred_element_type=jnp.float32
    )
    grad_gain_one = jnp.sum(grad_lowered_one * normed_one, 0)
    grad_shift_one = jnp.sum(grad_lowered_one, 0)
    grad_input = grad_resid + normalize_back(
        grad_lowered_one * gain_one.astype(jnp.float32), normed_one, inverse_one
    )
    grads = (
        grad_gain_one,
        grad_shift_one,
        grad_proj_mixed,
        grad_bias_query,
        grad_bias_value,
        grad_proj_out,
        grad_bias_out,
        grad_gain_two,
        grad_shift_two,
        grad_proj_up,
        grad_bias_up,
        grad_proj_down,
        grad_bias_down,
    )
    return (output, grad_input.astype(jnp.bfloat16), grads)


def fetch(shards):
    return (
        lax.all_gather(shards[0], "fsdp", axis=0, tiled=True),
        lax.all_gather(shards[1], "fsdp", axis=0, tiled=True),
        lax.all_gather(shards[2], "fsdp", axis=0, tiled=True),
        lax.all_gather(shards[3], "fsdp", axis=0, tiled=True),
        lax.all_gather(shards[4], "fsdp", axis=0, tiled=True),
        lax.all_gather(shards[5], "fsdp", axis=0, tiled=True),
        lax.all_gather(shards[6], "fsdp", axis=0, tiled=True),
        lax.all_gather(shards[7], "fsdp", axis=0, tiled=True),
        lax.all_gather(shards[8], "fsdp", axis=0, tiled=True),
        lax.all_gather(shards[9], "fsdp", axis=0, tiled=True),
        lax.all_gather(shards[10], "fsdp", axis=0, tiled=True),
        lax.all_gather(shards[11], "fsdp", axis=0, tiled=True),
        lax.all_gather(shards[12], "fsdp", axis=0, tiled=True),
    )


def share(grads):
    return (
        lax.psum_scatter(grads[0], "fsdp", scatter_dimension=0, tiled=True),
        lax.psum_scatter(grads[1], "fsdp", scatter_dimension=0, tiled=True),
        lax.psum_scatter(grads[2], "fsdp", scatter_dimension=0, tiled=True),
        lax.psum_scatter(grads[3], "fsdp", scatter_dimension=0, tiled=True),
        lax.psum_scatter(grads[4], "fsdp", scatter_dimension=0, tiled=True),
        lax.psum_scatter(grads[5], "fsdp", scatter_dimension=0, tiled=True),
        lax.psum_scatter(grads[6], "fsdp", scatter_dimension=0, tiled=True),
        lax.psum_scatter(grads[7], "fsdp", scatter_dimension=0, tiled=True),
        lax.psum_scatter(grads[8], "fsdp", scatter_dimension=0, tiled=True),
        lax.psum_scatter(grads[9], "fsdp", scatter_dimension=0, tiled=True),
        lax.psum_scatter(grads[10], "fsdp", scatter_dimension=0, tiled=True),
        lax.psum_scatter(grads[11], "fsdp", scatter_dimension=0, tiled=True),
        lax.psum_scatter(grads[12], "fsdp", scatter_dimension=0, tiled=True),
    )


def on_device(
    layer_input,
    segments,
    ln1_gain,
    ln1_bias,
    w_qkv,
    q_bias,
    v_bias,
    w_attn_out,
    b_attn_out,
    ln2_gain,
    ln2_bias,
    w_up,
    b_up,
    w_down,
    b_down,
    cotangent,
):
    shards = (
        ln1_gain,
        ln1_bias,
        w_qkv,
        q_bias,
        v_bias,
        w_attn_out,
        b_attn_out,
        ln2_gain,
        ln2_bias,
        w_up,
        b_up,
        w_down,
        b_down,
    )
    micro = layer_input.shape[0]
    count_rows = layer_input.shape[2]
    length = segments.shape[2]
    positions = stored_positions(length, lax.axis_size("ctx"))
    start = lax.axis_index("ctx") * count_rows
    outputs = []
    input_grads = []
    shared = None
    for number in range(micro):
        weights = fetch(shards)
        output, grad_input, grads = layer_pass(
            layer_input[number, 0],
            cotangent[number, 0],
            segments[number, 0],
            weights,
            positions,
            start,
        )
        summed = share(grads)
        shared = summed if shared is None else jax.tree.map(jnp.add, shared, summed)
        outputs.append(output)
        input_grads.append(grad_input)
    final = lax.psum(
        (
            shared[0],
            shared[1],
            shared[2],
            shared[3],
            shared[4],
            shared[5],
            shared[6],
            shared[7],
            shared[8],
            shared[9],
            shared[10],
            shared[11],
            shared[12],
        ),
        "ctx",
    )
    activations = jnp.stack(outputs)[:, None]
    input_grad = jnp.stack(input_grads)[:, None]
    return (
        activations,
        input_grad,
        final[0],
        final[1],
        final[2],
        final[3],
        final[4],
        final[5],
        final[6],
        final[7],
        final[8],
        final[9],
        final[10],
        final[11],
        final[12],
    )


def solution(mesh):
    in_specs = (
        P(None, "fsdp", "ctx", None),
        P(None, "fsdp", None),
        P("fsdp"),
        P("fsdp"),
        P("fsdp", None),
        P("fsdp"),
        P("fsdp"),
        P("fsdp", None),
        P("fsdp"),
        P("fsdp"),
        P("fsdp"),
        P("fsdp", None),
        P("fsdp"),
        P("fsdp", None),
        P("fsdp"),
        P(None, "fsdp", "ctx", None),
    )
    out_specs = (
        P(None, "fsdp", "ctx", None),
        P(None, "fsdp", "ctx", None),
        P("fsdp"),
        P("fsdp"),
        P("fsdp", None),
        P("fsdp"),
        P("fsdp"),
        P("fsdp", None),
        P("fsdp"),
        P("fsdp"),
        P("fsdp"),
        P("fsdp", None),
        P("fsdp"),
        P("fsdp", None),
        P("fsdp"),
    )
    return jax.shard_map(
        on_device, mesh=mesh, in_specs=in_specs, out_specs=out_specs, check_vma=False
    )
```

profile of v0, /device:TPU:0, one launch (start us, length us, event | category | flops | bytes accessed | tf_op | source)
XLA Modules:
  0.0 1276.0 jit_solution(1097453225849575975)
XLA Ops:
  18.2 63.6 %all-reduce.21 = (bf16[768]{0:T(1024)(128)(2,1)S(1)}, bf16[768]{0:T(1024)(128)(2,1)S(1)}, bf16[768]{0:T(1024)(128)(2,1)S(1)}, bf16[768]{0:T(1024)(128)(2,1)S(1)}...) all-reduce(bf16[768]{0:T(1024)(128)(2,1)S(1)} %dynamic-update-slice, ...), channel_id=1, replica_groups=mesh['ctx'=2,'fsdp'=16] {'fsdp'}, use_global_device_ids=true, to_apply=%add.3 | all-reduce | flops 9216 | bytes 36864
  84.1 4.2 fusion.157
  91.2 4.2 fusion.156
  104.0 29.5 %all-gather.17.cloned.1.call-done = bf16[1024,1536]{1,0:T(8,128)(2,1)} async-done(((bf16[512,1536]{1,0:T(8,128)(2,1)}), bf16[1024,1536]{1,0:T(8,128)(2,1)}) %all-gather.17.cloned.1.call-update) | async-done | bytes 3145744 | tf_op jit(solution)/shard_map/all_gather | solution.py:178
  133.5 3.8 fusion.249
  146.1 3.9 reshape.537
  152.9 30.9 %while.84 = (s32[]{:T(128)}, f32[12,512]{1,0:T(8,128)S(1)}, f32[12,512]{1,0:T(8,128)S(1)}, f32[512,12,64]{0,2,1:T(8,128)}, s32[2,512]{1,0:T(2,128)S(1)}, /*index...) while((s32[]{:T(128)}, f32[12,512]{1,0:T(8,128)S(1)}, ...), condition=%wide.region_15.16_spmd.clone, body=%wide.region_12.15_spmd.clone.sunk | while | flops 1276416000 | bytes 80412920 | solution.py:76
  159.7 3.4 fusion.367
  163.1 4.1 bitcast_add_fusion.14
  175.1 3.4 fusion.367
  178.6 4.1 bitcast_add_fusion.14
  183.8 4.3 fusion.248
  196.6 3.8 reshape.534
  203.3 29.1 %while.82 = (s32[]{:T(128)}, f32[12,512]{1,0:T(8,128)S(1)}, f32[12,512]{1,0:T(8,128)S(1)}, f32[512,12,64]{0,2,1:T(8,128)}, s32[2,512]{1,0:T(2,128)S(1)}, /*index...) while((s32[]{:T(128)}, f32[12,512]{1,0:T(8,128)S(1)}, ...), condition=%wide.region_5.6_spmd.clone, body=%wide.region_2.5_spmd.clone.sunk | while | flops 1276416000 | bytes 80412920 | solution.py:76
  209.3 3.4 fusion.354
  212.7 4.1 bitcast_add_fusion.12
  227.1 4.1 bitcast_add_fusion.12
  232.4 15.4 %while.85 = (s32[]{:T(128)}, f32[512,12,64]{0,2,1:T(8,128)}, bf16[2,512,12,64]{1,3,2,0:T(8,128)(2,1)}, s32[2,512]{1,0:T(2,128)S(1)}, s32[512]{0:T(512)S(1)}, /*i...) while((s32[]{:T(128)}, f32[512,12,64]{0,2,1:T(8,128)}, ...), condition=%wide.region_17.18_spmd.clone, body=%wide.region_16.17_spmd.clone.sunk | while | flops 822607872 | bytes 6071946 | solution.py:97
  232.7 7.1 bitcast_add_fusion.15
  240.1 7.7 bitcast_add_fusion.15
  251.1 14.5 %while.83 = (s32[]{:T(128)}, f32[512,12,64]{0,2,1:T(8,128)}, bf16[2,512,12,64]{1,3,2,0:T(8,128)(2,1)}, s32[2,512]{1,0:T(2,128)S(1)}, s32[512]{0:T(512)S(1)}, /*i...) while((s32[]{:T(128)}, f32[512,12,64]{0,2,1:T(8,128)}, ...), condition=%wide.region_7.8_spmd.clone, body=%wide.region_6.7_spmd.clone.sunk | while | flops 822607872 | bytes 6080138 | solution.py:97
  251.6 6.6 bitcast_add_fusion.13
  258.4 7.1 bitcast_add_fusion.13
  275.2 8.3 fusion.246
  283.5 4.8 fusion.247
  288.3 40.8 %all-gather.15.cloned.1.call-done = bf16[3072,768]{1,0:T(8,128)(2,1)} async-done(((bf16[192,768]{1,0:T(8,128)(2,1)}), bf16[3072,768]{1,0:T(8,128)(2,1)}) %all-gather.15.cloned.1.call-update) | async-done | bytes 4718608 | tf_op jit(solution)/shard_map/all_gather | solution.py:292
  329.2 10.7 convert_reduce_fusion.1
  339.9 7.1 convert_reduce_fusion
  349.8 4.0 multiply_reduce_fusion.1
  367.3 164.6 %while.87 = (s32[]{:T(128)}, f32[512,12,64]{0,2,1:T(8,128)}, f32[2,512,12,64]{1,0,3,2:T(2,128)}, f32[2,512,12,64]{1,0,3,2:T(2,128)}, bf16[2,512,12,64]{1,3,2,0:T...) while((s32[]{:T(128)}, f32[512,12,64]{0,2,1:T(8,128)}, ...), condition=%wide.region_30.31_spmd.clone, body=%wide.region_29.30_spmd.clone.sunk | while | flops 2053373952 | bytes 100753672 | solution.py:129
  371.0 5.4 fusion.397
  376.4 5.8 fusion.396
  386.6 3.7 multiply_bitcast_fusion.5
  392.0 28.8 %dynamic_update_slice.23 = f32[2,512,12,64]{1,0,3,2:T(2,128)} dynamic-update-slice(f32[2,512,12,64]{1,0,3,2:T(2,128)} %get-tuple-element.1775, f32[1,512,12,64]{1,0,3,2:T(1,128)S(1)} %copy.219, s32[]{:T(128)S(6)} %copy.274, s32[]{:T(128)} %constant.199.clone.1..sunk.5, s32[]{:T(128)} %constant.199.clone.1..sunk.5, s32[]{:T(128)} %constant.199.clone.1..sunk.5) | dynamic-update-slice | bytes 3145732 | tf_op jit(solution)/shard_map/while/body/jit(dynamic_update_index_in_dim)/dynamic_update_slice | solution.py:129
  420.8 28.8 %dynamic_update_slice.24 = f32[2,512,12,64]{1,0,3,2:T(2,128)} dynamic-update-slice(f32[2,512,12,64]{1,0,3,2:T(2,128)} %get-tuple-element.1776, f32[1,512,12,64]{1,0,3,2:T(1,128)S(1)} %copy.220, s32[]{:T(128)S(6)} %copy.274, s32[]{:T(128)} %constant.199.clone.1..sunk.5, s32[]{:T(128)} %constant.199.clone.1..sunk.5, s32[]{:T(128)} %constant.199.clone.1..sunk.5) | dynamic-update-slice | bytes 3145732 | tf_op jit(solution)/shard_map/while/body/jit(dynamic_update_index_in_dim)/dynamic_update_slice | solution.py:129
  453.1 5.4 fusion.397
  458.4 5.8 fusion.396
  468.7 3.7 multiply_bitcast_fusion.5
  474.0 28.8 %dynamic_update_slice.23 = f32[2,512,12,64]{1,0,3,2:T(2,128)} dynamic-update-slice(f32[2,512,12,64]{1,0,3,2:T(2,128)} %get-tuple-element.1775, f32[1,512,12,64]{1,0,3,2:T(1,128)S(1)} %copy.219, s32[]{:T(128)S(6)} %copy.274, s32[]{:T(128)} %constant.199.clone.1..sunk.5, s32[]{:T(128)} %constant.199.clone.1..sunk.5, s32[]{:T(128)} %constant.199.clone.1..sunk.5) | dynamic-update-slice | bytes 3145732 | tf_op jit(solution)/shard_map/while/body/jit(dynamic_update_index_in_dim)/dynamic_update_slice | solution.py:129
  502.8 28.8 %dynamic_update_slice.24 = f32[2,512,12,64]{1,0,3,2:T(2,128)} dynamic-update-slice(f32[2,512,12,64]{1,0,3,2:T(2,128)} %get-tuple-element.1776, f32[1,512,12,64]{1,0,3,2:T(1,128)S(1)} %copy.220, s32[]{:T(128)S(6)} %copy.274, s32[]{:T(128)} %constant.199.clone.1..sunk.5, s32[]{:T(128)} %constant.199.clone.1..sunk.5, s32[]{:T(128)} %constant.199.clone.1..sunk.5) | dynamic-update-slice | bytes 3145732 | tf_op jit(solution)/shard_map/while/body/jit(dynamic_update_index_in_dim)/dynamic_update_slice | solution.py:129
  551.1 165.4 %while.86 = (s32[]{:T(128)}, f32[512,12,64]{0,2,1:T(8,128)}, f32[2,512,12,64]{1,0,3,2:T(2,128)}, f32[2,512,12,64]{1,0,3,2:T(2,128)}, bf16[2,512,12,64]{1,3,2,0:T...) while((s32[]{:T(128)}, f32[512,12,64]{0,2,1:T(8,128)}, ...), condition=%wide.region_23.24_spmd.clone, body=%wide.region_22.23_spmd.clone.sunk | while | flops 2053373952 | bytes 110190944 | solution.py:129
  555.5 5.5 fusion.384
  560.9 5.8 fusion.383
  576.0 28.9 %dynamic_update_slice.21 = f32[2,512,12,64]{1,0,3,2:T(2,128)} dynamic-update-slice(f32[2,512,12,64]{1,0,3,2:T(2,128)} %get-tuple-element.1823, f32[1,512,12,64]{1,0,3,2:T(1,128)} %copy.217, s32[]{:T(128)S(6)} %copy.286, s32[]{:T(128)} %constant.199.clone.1..sunk.4, s32[]{:T(128)} %constant.199.clone.1..sunk.4, s32[]{:T(128)} %constant.199.clone.1..sunk.4) | dynamic-update-slice | bytes 3145732 | tf_op jit(solution)/shard_map/while/body/jit(dynamic_update_index_in_dim)/dynamic_update_slice | solution.py:129
  604.9 28.8 %dynamic_update_slice.22 = f32[2,512,12,64]{1,0,3,2:T(2,128)} dynamic-update-slice(f32[2,512,12,64]{1,0,3,2:T(2,128)} %get-tuple-element.1824, f32[1,512,12,64]{1,0,3,2:T(1,128)S(1)} %copy.218, s32[]{:T(128)S(6)} %copy.286, s32[]{:T(128)} %constant.199.clone.1..sunk.4, s32[]{:T(128)} %constant.199.clone.1..sunk.4, s32[]{:T(128)} %constant.199.clone.1..sunk.4) | dynamic-update-slice | bytes 3145732 | tf_op jit(solution)/shard_map/while/body/jit(dynamic_update_index_in_dim)/dynamic_update_slice | solution.py:129
  638.1 5.4 fusion.384
  643.5 5.8 fusion.383
  658.6 28.9 %dynamic_update_slice.21 = f32[2,512,12,64]{1,0,3,2:T(2,128)} dynamic-update-slice(f32[2,512,12,64]{1,0,3,2:T(2,128)} %get-tuple-element.1823, f32[1,512,12,64]{1,0,3,2:T(1,128)} %copy.217, s32[]{:T(128)S(6)} %copy.286, s32[]{:T(128)} %constant.199.clone.1..sunk.4, s32[]{:T(128)} %constant.199.clone.1..sunk.4, s32[]{:T(128)} %constant.199.clone.1..sunk.4) | dynamic-update-slice | bytes 3145732 | tf_op jit(solution)/shard_map/while/body/jit(dynamic_update_index_in_dim)/dynamic_update_slice | solution.py:129
  687.5 28.8 %dynamic_update_slice.22 = f32[2,512,12,64]{1,0,3,2:T(2,128)} dynamic-update-slice(f32[2,512,12,64]{1,0,3,2:T(2,128)} %get-tuple-element.1824, f32[1,512,12,64]{1,0,3,2:T(1,128)S(1)} %copy.218, s32[]{:T(128)S(6)} %copy.286, s32[]{:T(128)} %constant.199.clone.1..sunk.4, s32[]{:T(128)} %constant.199.clone.1..sunk.4, s32[]{:T(128)} %constant.199.clone.1..sunk.4) | dynamic-update-slice | bytes 3145732 | tf_op jit(solution)/shard_map/while/body/jit(dynamic_update_index_in_dim)/dynamic_update_slice | solution.py:129
  730.3 5.9 fusion.206
  736.3 10.1 convolution_add_fusion.1
  747.8 5.2 fusion.245
  753.0 6.1 convolution_add_fusion.2
  764.7 34.2 %reduce-scatter.7.cloned.1.call-done = f32[512,1536]{0,1:T(8,128)} async-done(((f32[1024,1536]{0,1:T(8,128)}), f32[512,1536]{0,1:T(8,128)}) %reduce-scatter.7.cloned.1.call-update) | async-done | bytes 3145744 | tf_op jit(solution)/shard_map/reduce_scatter | solution.py:244
  803.6 5.3 convolution_add_fusion
  810.8 9.1 fusion.197
  819.9 8.4 fusion.198
  832.8 4.3 fusion.190
  837.2 28.5 %reduce-scatter.13.cloned.1.call-done = f32[48,768]{1,0:T(8,128)} async-done(((f32[768,768]{1,0:T(8,128)}), f32[48,768]{1,0:T(8,128)}) %reduce-scatter.13.cloned.1.call-update) | async-done | bytes 147472 | tf_op jit(solution)/shard_map/reduce_scatter | solution.py:304
  865.7 114.9 %reduce-scatter.17.cloned.1.call-done = f32[192,768]{1,0:T(8,128)} async-done(((f32[3072,768]{1,0:T(8,128)}), f32[192,768]{1,0:T(8,128)}) %reduce-scatter.17.cloned.1.call-update) | async-done | bytes 589840 | tf_op jit(solution)/shard_map/reduce_scatter | solution.py:310
  980.6 115.2 %reduce-scatter.15.cloned.1.call-done = f32[48,3072]{1,0:T(8,128)} async-done(((f32[768,3072]{1,0:T(8,128)}), f32[48,3072]{1,0:T(8,128)}) %reduce-scatter.15.cloned.1.call-update) | async-done | bytes 589840 | tf_op jit(solution)/shard_map/reduce_scatter | solution.py:308
  1095.9 94.2 %reduce-scatter.11.cloned.1.call-done = f32[48,2304]{1,0:T(8,128)} async-done(((f32[768,2304]{1,0:T(8,128)}), f32[48,2304]{1,0:T(8,128)}) %reduce-scatter.11.cloned.1.call-update) | async-done | bytes 442384 | tf_op jit(solution)/shard_map/reduce_scatter | solution.py:301
  1192.7 59.6 %all-reduce.18 = (f32[768]{0:T(1024)S(1)}, f32[768]{0:T(1024)S(1)}, f32[768]{0:T(1024)S(1)}, f32[768]{0:T(1024)S(1)}, f32[768]{0:T(1024)S(1)}, /*index=5*/f32[76...) all-reduce(f32[768]{0:T(1024)S(1)} %add.461, ...), channel_id=17, replica_groups=mesh['ctx'=2,'fsdp'=16] {'fsdp'}, use_global_device_ids=true, to_apply=%region_35.36.clone | all-reduce | flops 9216 | bytes 73728
  1253.0 5.6 all-reduce.19
  (497 shorter events, 217.7 us)
Async XLA Ops:
  7.2 76.3 %copy-start.12 = (bf16[2,1,512,768]{3,2,1,0:T(8,128)(2,1)S(1)}, bf16[2,1,512,768]{3,2,1,0:T(8,128)(2,1)}, u32[]{:S(2)}) copy-start(bf16[2,1,512,768]{3,2,1,0:T(8,128)(2,1)} %param.28) | copy-start | bytes 4718596
  7.2 76.9 %all-gather.7.cloned.1.call-start = ((), (), s32[]{:S(2)}) async-start(), calls=%async_computation.6 | async-start | bytes 3760128 | tf_op jit(solution)/shard_map/all_gather | solution.py:283
  7.9 125.5 %all-gather.17.cloned.1.call-start = ((), (), s32[]{:S(2)}) async-start(), calls=%async_computation.11 | async-start | bytes 4718592 | tf_op jit(solution)/shard_map/all_gather | solution.py:178
  81.7 9.4 copy-start.65
  81.7 9.4 copy-start.69
  83.4 4.8 copy-start.73
  83.4 7.7 copy-start.84
  84.1 4.2 copy-start.75
  91.1 92.8 %all-gather.9.cloned.1.call-start = ((), (), s32[]{:S(2)}) async-start(), calls=%async_computation.7 | async-start | bytes 4718592 | tf_op jit(solution)/shard_map/all_gather | solution.py:178
  91.1 4.2 copy-start.94
  96.7 5.7 copy-start.98
  98.1 4.5 slice-start
  98.1 170.8 %all-gather.11.cloned.1.call-start = ((), (), s32[]{:S(2)}) async-start(), calls=%async_computation.8 | async-start | bytes 1253376 | tf_op jit(solution)/shard_map/all_gather | solution.py:286
  98.7 176.5 %all-gather.13.cloned.1.call-start = ((), (), s32[]{:S(2)}) async-start(), calls=%async_computation.9 | async-start | bytes 5013504 | tf_op jit(solution)/shard_map/all_gather | solution.py:290
  99.2 229.9 %all-gather.15.cloned.1.call-start = ((), (), s32[]{:S(2)}) async-start(), calls=%async_computation.10 | async-start | bytes 5013504 | tf_op jit(solution)/shard_map/all_gather | solution.py:292
  99.8 662.7 %reduce-scatter.9.cloned.1.call-start = ((), (), s32[]{:S(2)}) async-start(), calls=%async_computation.13 | async-start | bytes 9437184 | tf_op jit(solution)/shard_map/reduce_scatter | solution.py:244
  175.1 3.4 copy-start.52
  183.8 4.3 copy-start.4
  232.3 18.0 %copy-start.43 = (f32[12,512]{1,0:T(8,128)}, f32[12,512]{1,0:T(8,128)S(1)}, u32[]{:S(2)}) copy-start(f32[12,512]{1,0:T(8,128)S(1)} %get-tuple-element.386) | copy-start | bytes 73732
  250.3 18.5 %copy-start.36 = (bf16[512,12,64]{0,2,1:T(8,128)(2,1)}, bf16[512,12,64]{0,2,1:T(8,128)(2,1)S(1)}, u32[]{:S(2)}) copy-start(bf16[512,12,64]{0,2,1:T(8,128)(2,1)S(1)} %convert_element_type.212) | copy-start | bytes 2359300
  265.5 5.9 copy-start
  265.5 5.9 copy-start.59
  265.6 5.9 copy-start.61
  265.6 7.2 copy-start.2
  271.5 82.3 %copy-start.71 = (f32[512]{0:T(512)}, f32[512]{0:T(512)S(1)}, u32[]{:S(2)}) copy-start(f32[512]{0:T(512)S(1)} %broadcast_multiply_fusion.8) | copy-start | bytes 6148
  272.8 81.0 %copy-start.82 = (f32[512]{0:T(512)}, f32[512]{0:T(512)S(1)}, u32[]{:S(2)}) copy-start(f32[512]{0:T(512)S(1)} %broadcast_multiply_fusion.10) | copy-start | bytes 6148
  274.0 79.8 %copy-start.77 = (f32[512]{0:T(512)}, f32[512]{0:T(512)S(1)}, u32[]{:S(2)}) copy-start(f32[512]{0:T(512)S(1)} %add_rsqrt_fusion) | copy-start | bytes 6148
  274.0 79.8 %copy-start.96 = (f32[512]{0:T(512)}, f32[512]{0:T(512)S(1)}, u32[]{:S(2)}) copy-start(f32[512]{0:T(512)S(1)} %add_rsqrt_fusion.2) | copy-start | bytes 6148
  274.0 9.5 copy-start.16
  275.2 8.4 copy-start.106
  283.5 45.6 %copy-start.45 = (bf16[2,1,512,768]{3,2,1,0:T(8,128)(2,1)S(1)}, bf16[2,1,512,768]{3,2,1,0:T(8,128)(2,1)}, u32[]{:S(2)}) copy-start(bf16[2,1,512,768]{3,2,1,0:T(8,128)(2,1)} %param.43) | copy-start | bytes 4718596
  283.5 45.6 %copy-start.90 = (f32[3072]{0:T(1024)S(1)}, f32[3072]{0:T(1024)}, u32[]{:S(2)}) copy-start(f32[3072]{0:T(1024)} %convert_element_type.204) | copy-start | bytes 36868
  329.1 10.7 copy-start.105
  329.1 10.7 copy-start.110
  329.1 17.9 %slice-start.2 = ((s8[4718592]{0:T(1024)(128)(4,1)}), s8[4194304]{0:T(1024)(128)(4,1)S(1)}, s32[]{:S(2)}) async-start(s8[4718592]{0:T(1024)(128)(4,1)} %bitcast.596), calls=%async_computation.21 | async-start | bytes 8388608
  339.9 9.9 copy-start.111
  339.9 7.1 slice-start.3
  353.8 4.3 copy-start.109
  386.6 3.7 copy-start.7
  468.7 3.7 copy-start.7
  538.8 260.1 %reduce-scatter.7.cloned.1.call-start = ((), (), s32[]{:S(2)}) async-start(), calls=%async_computation.12 | async-start | bytes 9437184 | tf_op jit(solution)/shard_map/reduce_scatter | solution.py:244
  540.2 4.8 copy-start.44
  540.2 4.8 copy-start.51
  604.9 28.9 %copy-start.42 = (bf16[512,12,64]{0,2,1:T(8,128)(2,1)S(1)}, bf16[512,12,64]{0,2,1:T(8,128)(2,1)}, u32[]{:S(2)}) copy-start(bf16[512,12,64]{0,2,1:T(8,128)(2,1)} %copy-done.41) | copy-start | bytes 2359300 | tf_op jit(solution)/shard_map/while
  687.5 28.9 %copy-start.42 = (bf16[512,12,64]{0,2,1:T(8,128)(2,1)S(1)}, bf16[512,12,64]{0,2,1:T(8,128)(2,1)}, u32[]{:S(2)}) copy-start(bf16[512,12,64]{0,2,1:T(8,128)(2,1)} %copy-done.41) | copy-start | bytes 2359300 | tf_op jit(solution)/shard_map/while
  723.3 142.4 %reduce-scatter.13.cloned.1.call-start = ((), (), s32[]{:S(2)}) async-start(), calls=%async_computation.15 | async-start | bytes 2506752 | tf_op jit(solution)/shard_map/reduce_scatter | solution.py:304
  728.9 251.7 %reduce-scatter.17.cloned.1.call-start = ((), (), s32[]{:S(2)}) async-start(), calls=%async_computation.17 | async-start | bytes 10027008 | tf_op jit(solution)/shard_map/reduce_scatter | solution.py:310
  746.4 6.6 copy-start.17
  746.4 6.6 copy-start.72
  746.4 6.6 copy-start.78
  746.5 349.4 %reduce-scatter.15.cloned.1.call-start = ((), (), s32[]{:S(2)}) async-start(), calls=%async_computation.16 | async-start | bytes 10027008 | tf_op jit(solution)/shard_map/reduce_scatter | solution.py:308
  747.8 5.2 copy-start.35
  759.2 430.9 %reduce-scatter.11.cloned.1.call-start = ((), (), s32[]{:S(2)}) async-start(), calls=%async_computation.14 | async-start | bytes 7520256 | tf_op jit(solution)/shard_map/reduce_scatter | solution.py:301
  764.6 64.9 %copy-start.26 = (bf16[512,1536]{0,1:T(8,128)(2,1)}, bf16[512,1536]{0,1:T(8,128)(2,1)S(1)}, u32[]{:S(2)}) copy-start(bf16[512,1536]{0,1:T(8,128)(2,1)S(1)} %convert.17) | copy-start | bytes 4718596
  764.7 36.4 %copy-start.14 = (bf16[2,1,512,768]{3,2,1,0:T(8,128)(2,1)S(1)}, bf16[2,1,512,768]{3,2,1,0:T(8,128)(2,1)}, u32[]{:S(2)}) copy-start(bf16[2,1,512,768]{3,2,1,0:T(8,128)(2,1)} %param.28) | copy-start | bytes 4718596
  764.7 36.4 %copy-start.66 = (f32[768]{0:T(1024)S(1)}, f32[768]{0:T(1024)}, u32[]{:S(2)}) copy-start(f32[768]{0:T(1024)} %copy-done.65) | copy-start | bytes 9220
  764.7 36.4 %copy-start.70 = (f32[768]{0:T(1024)S(1)}, f32[768]{0:T(1024)}, u32[]{:S(2)}) copy-start(f32[768]{0:T(1024)} %copy-done.69) | copy-start | bytes 9220
  764.7 36.4 %copy-start.85 = (f32[512]{0:T(512)S(1)}, f32[512]{0:T(512)}, u32[]{:S(2)}) copy-start(f32[512]{0:T(512)} %copy-done.84) | copy-start | bytes 6148
  764.7 36.4 %copy-start.95 = (f32[512]{0:T(512)S(1)}, f32[512]{0:T(512)}, u32[]{:S(2)}) copy-start(f32[512]{0:T(512)} %copy-done.94) | copy-start | bytes 6148
  809.0 453.8 %all-reduce.24.cloned.1.call-start = ((), (), s32[]{:S(2)}) async-start(), calls=%async_computation.18 | async-start | bytes 3538944 | tf_op jit(solution)/shard_map/psum | solution.py:370
  810.8 9.1 copy-start.18
  819.9 9.7 copy-start.107
  837.2 421.4 %copy-start.21 = (f32[512,768]{1,0:T(8,128)S(1)}, f32[512,768]{1,0:T(8,128)}, u32[]{:S(2)}) copy-start(f32[512,768]{1,0:T(8,128)} %copy-done.19) | copy-start | bytes 4718596
  1262.9 5.4 copy-start.58
  (80 other events, 175.5 us)
Sparse Core Ops, SparseCore 0:
  10.3 50.3 all-gather.6
  91.2 42.2 all-gather.16
  135.0 44.9 all-gather.8
  182.1 38.3 all-gather.10
  222.6 52.4 all-gather.12
  277.3 51.7 all-gather.14
  538.9 75.5 reduce-scatter.8
  723.4 75.4 reduce-scatter.6
  802.7 62.9 reduce-scatter.12
  870.2 110.3 reduce-scatter.16
  984.7 111.0 reduce-scatter.14
  1100.2 89.7 reduce-scatter.10
  1192.5 55.8 all-reduce.23
where the time goes:
time: 1300 us; the launch traced here: 1280 us
  waiting for transfers between devices  461 us (35%)
  local copies, waits for them, and re-layouts  353 us (27%)
  matrix products  259 us (20%)
  blocking collectives  129 us (10%)
  other arithmetic  53.1 us (4%)
  between operations  18.4 us (1%)
    dynamic_update_slice x16, local copies, waits for them, and re-layouts, attention_back(): lax.scan(advance, jnp.zeros(query.shape, jnp.float32), tiles)  252 us
    unnamed x2, blocking collectives  123 us
    reduce_scatter x1, waiting for transfers between devices, share(): lax.psum_scatter(grads[9], 'fsdp', scatter_dimension=0, tiled=True)  115 us
    reduce_scatter x1, waiting for transfers between devices, share(): lax.psum_scatter(grads[11], 'fsdp', scatter_dimension=0, tiled=True)  115 us
    reduce_scatter x1, waiting for transfers between devices, share(): lax.psum_scatter(grads[2], 'fsdp', scatter_dimension=0, tiled=True)  94.2 us
    unnamed x238, local copies, waits for them, and re-layouts  45.8 us
    all_gather x1, waiting for transfers between devices, fetch(): lax.all_gather(shards[11], 'fsdp', axis=0, tiled=True)  40.8 us
    reduce_scatter x2, waiting for transfers between devices, layer_pass(): lax.psum_scatter(grad_pairs, 'ctx', scatter_dimension=0, tiled=True)  34.2 us
  transfers between devices with their start and end apart: 13, of which 8 were waited for; matrix products, arithmetic and copies ran while one was open for 33% of the time, Pallas kernels for 0%

commit v1 on v0

--- a/solution.py
+++ b/solution.py
@@ -1,6 +1,8 @@
 import jax
 import jax.numpy as jnp
 from jax import lax
+from jax.experimental import pallas as pl
+from jax.experimental.pallas import tpu as pltpu
 from jax.sharding import PartitionSpec as P
 
 H = 12
@@ -406,6 +408,380 @@
     )
 
 
+D = 768
+HD = 64
+BLK = 256
+NEG = -1e30
+F32 = jnp.float32
+BF16 = jnp.bfloat16
+
+
+def dot(lhs, rhs, lhs_dim, rhs_dim):
+    return lax.dot_general(
+        lhs, rhs, (((lhs_dim,), (rhs_dim,)), ((), ())), preferred_element_type=F32
+    )
+
+
+def norm(v):
+    center = v - jnp.mean(v, -1, keepdims=True)
+    inverse = lax.rsqrt(jnp.mean(center * center, -1, keepdims=True) + 1e-05)
+    return center * inverse, inverse
+
+
+def colsum(v):
+    return jnp.sum(v, 0, keepdims=True)
+
+
+def loop(count, body):
+    def step(index, carry):
+        body(index)
+        return carry
+
+    lax.fori_loop(0, count, step, 0)
+
+
+def lanes(index, size):
+    return pl.ds(pl.multiple_of(index * size, size), size)
+
+
+def attention_masks(seg_ref, bias_ref, mine):
+    key = lax.broadcasted_iota(jnp.int32, (BLK, BLK), 0)
+    query = lax.broadcasted_iota(jnp.int32, (BLK, BLK), 1)
+    causal = key <= query
+    for micro in range(2):
+
+        def row(start):
+            piece = seg_ref[micro : micro + 1, pl.ds(pl.multiple_of(start, BLK), BLK)]
+            return jnp.broadcast_to(piece.astype(F32), (BLK, BLK))
+
+        solo = row(mine * 2 * BLK + mine * BLK)
+        wide = row(mine * 2 * BLK + (1 - mine) * BLK)
+        extra = row((1 - mine) * 3 * BLK)
+        bias_ref[micro, 0:BLK] = jnp.where((solo.T == solo) & causal, 0.0, NEG)
+        bias_ref[micro, BLK : 2 * BLK] = jnp.where(extra.T == wide, 0.0, NEG)
+        bias_ref[micro, 2 * BLK :] = jnp.where((wide.T == wide) & causal, 0.0, NEG)
+
+
+def attention_rows(micro, mine):
+    solo = pl.ds(pl.multiple_of(micro * 2 * BLK + mine * BLK, BLK), BLK)
+    wide = pl.ds(pl.multiple_of(micro * 2 * BLK + (1 - mine) * BLK, BLK), BLK)
+    extra = pl.ds(pl.multiple_of(1024 + micro * BLK, BLK), BLK)
+    return solo, wide, extra
+
+
+def halves(value):
+    left = lax.broadcasted_iota(jnp.int32, value.shape, 1) < HD
+    zero = jnp.zeros_like(value)
+    return jnp.where(left, value, zero), jnp.where(left, zero, value)
+
+
+def softmax_columns(tiles):
+    peak = tiles[0].max(0, keepdims=True)
+    for tile in tiles[1:]:
+        peak = jnp.maximum(peak, tile.max(0, keepdims=True))
+    terms = [jnp.exp(tile - peak) for tile in tiles]
+    total = colsum(terms[0])
+    for term in terms[1:]:
+        total = total + colsum(term)
+    scale = 1.0 / total
+    return [(term * scale).astype(BF16) for term in terms]
+
+
+def attention_forward(index, refs, mine):
+    q_ref, k_ref, v_ref, o_ref, p_ref, bias_ref = refs
+    micro = index // 6
+    pair = lanes(index % 6, 128)
+    solo, wide, extra = attention_rows(micro, mine)
+    k_s, k_x, k_e = k_ref[solo, pair], k_ref[wide, pair], k_ref[extra, pair]
+    vt_s, vt_x, vt_e = v_ref[solo, pair].T, v_ref[wide, pair].T, v_ref[extra, pair].T
+    q_s, q_x = halves(q_ref[solo, pair]), halves(q_ref[wide, pair])
+    outs_s, outs_x = [], []
+    for head in range(2):
+        rows = slice(head * HD, head * HD + HD)
+        (p_s,) = softmax_columns([dot(k_s, q_s[head], 1, 1) + bias_ref[micro, 0:BLK]])
+        p_e, p_x = softmax_columns(
+            [
+                dot(k_e, q_x[head], 1, 1) + bias_ref[micro, BLK : 2 * BLK],
+                dot(k_x, q_x[head], 1, 1) + bias_ref[micro, 2 * BLK :],
+            ]
+        )
+        p_ref[index, head, 0:BLK] = p_s
+        p_ref[index, head, BLK : 2 * BLK] = p_e
+        p_ref[index, head, 2 * BLK :] = p_x
+        outs_s.append(dot(vt_s[rows], p_s, 1, 0))
+        outs_x.append(dot(vt_e[rows], p_e, 1, 0) + dot(vt_x[rows], p_x, 1, 0))
+    o_ref[solo, pair] = jnp.concatenate(outs_s, 0).T.astype(BF16)
+    o_ref[wide, pair] = jnp.concatenate(outs_x, 0).T.astype(BF16)
+
+
+def attention_backward(index, refs, mine):
+    q_ref, k_ref, v_ref, go_ref, p_ref = refs
+    micro = index // 6
+    pair = lanes(index % 6, 128)
+    solo, wide, extra = attention_rows(micro, mine)
+    k_s, k_x, k_e = k_ref[solo, pair], k_ref[wide, pair], k_ref[extra, pair]
+    v_s, v_x, v_e = v_ref[solo, pair], v_ref[wide, pair], v_ref[extra, pair]
+    kt_s, kt_x, kt_e = k_s.T, k_x.T, k_e.T
+    q_s, q_x = halves(q_ref[solo, pair]), halves(q_ref[wide, pair])
+    go_s, go_x = halves(go_ref[solo, pair]), halves(go_ref[wide, pair])
+    p_all, g_all, outs_s, outs_x = [], [], [], []
+    for head in range(2):
+        rows = slice(head * HD, head * HD + HD)
+        p_s, p_e, p_x = (p_ref[index, head, BLK * t : BLK * t + BLK] for t in range(3))
+        f_s, f_e, f_x = p_s.astype(F32), p_e.astype(F32), p_x.astype(F32)
+        t_s = f_s * dot(v_s, go_s[head], 1, 1)
+        t_e = f_e * dot(v_e, go_x[head], 1, 1)
+        t_x = f_x * dot(v_x, go_x[head], 1, 1)
+        d_s = colsum(t_s)
+        d_x = colsum(t_e) + colsum(t_x)
+        g_s = (t_s - f_s * d_s).astype(BF16)
+        g_e = (t_e - f_e * d_x).astype(BF16)
+        g_x = (t_x - f_x * d_x).astype(BF16)
+        outs_s.append(dot(kt_s[rows], g_s, 1, 0))
+        outs_x.append(dot(kt_e[rows], g_e, 1, 0) + dot(kt_x[rows], g_x, 1, 0))
+        p_all.append((p_s, p_e, p_x))
+        g_all.append((g_s, g_e, g_x))
+
+    def both(tiles, which, right):
+        return dot(jnp.concatenate([tiles[0][which], tiles[1][which]], 1), right, 1, 0).astype(BF16)
+
+    go_s, go_x = jnp.concatenate(go_s, 0), jnp.concatenate(go_x, 0)
+    q_s, q_x = jnp.concatenate(q_s, 0), jnp.concatenate(q_x, 0)
+    v_ref[solo, pair] = both(p_all, 0, go_s)
+    v_ref[extra, pair] = both(p_all, 1, go_x)
+    v_ref[wide, pair] = both(p_all, 2, go_x)
+    k_ref[solo, pair] = both(g_all, 0, q_s)
+    k_ref[extra, pair] = both(g_all, 1, q_x)
+    k_ref[wide, pair] = both(g_all, 2, q_x)
+    q_ref[solo, pair] = (jnp.concatenate(outs_s, 0).T * 0.125).astype(BF16)
+    q_ref[wide, pair] = (jnp.concatenate(outs_x, 0).T * 0.125).astype(BF16)
+
+
+def layer_kernel(
+    x_hbm, xe_hbm, cot_hbm, seg_ref, w_hbm, vec_ref, act_hbm, g1_hbm, gr_hbm, g1e_hbm, g_hbm, vg_hbm,
+    w_ref, x_ref, cot_ref, q_ref, k_ref, v_ref, o_ref, p_ref, bias_ref, acc_ref, n2_ref, a2_ref, rs2_ref,
+    g2_ref, a1_ref, a3_ref, gu_ref, vg_ref, bup_ref, sem,
+):
+    mine = lax.axis_index("ctx")
+    for i, (src, dst) in enumerate(
+        ((x_hbm, x_ref.at[0:1024]), (xe_hbm, x_ref.at[1024:1536]), (cot_hbm, cot_ref), (w_hbm, w_ref))
+    ):
+        pltpu.make_async_copy(src, dst, sem.at[i]).start()
+    for i, (src, dst) in enumerate(
+        ((x_hbm, x_ref.at[0:1024]), (xe_hbm, x_ref.at[1024:1536]), (cot_hbm, cot_ref), (w_hbm, w_ref))
+    ):
+        pltpu.make_async_copy(src, dst, sem.at[i]).wait()
+
+    def weight(index):
+        return w_ref[index].reshape(D, D)
+
+    def vec(row):
+        return vec_ref[row : row + 1, :].astype(F32)
+
+    vg_ref[...] = jnp.zeros_like(vg_ref)
+
+    def add_vec(row, value):
+        vg_ref[row : row + 1, :] += value
+
+    def first_norm(r):
+        rows = pl.ds(r * BLK, BLK)
+        normed, _ = norm(x_ref[rows, :].astype(F32))
+        a1_ref[rows, :] = (normed * vec(0) + vec(1)).astype(BF16)
+
+    loop(6, first_norm)
+    attention_masks(seg_ref, bias_ref, mine)
+    k_ref[...] = dot(a1_ref[...], weight(1), 1, 0).astype(BF16)
+    v_ref[...] = (dot(a1_ref[...], weight(2), 1, 0) + vec(3)).astype(BF16)
+    q_ref[...] = ((dot(a1_ref[0:1024, :], weight(0), 1, 0) + vec(2)).astype(BF16) * 0.125).astype(BF16)
+    loop(12, lambda i: attention_forward(i, (q_ref, k_ref, v_ref, o_ref, p_ref, bias_ref), mine))
+
+    acc_ref[...] = dot(o_ref[...], weight(3), 1, 0)
+
+    def second_norm(r):
+        rows = pl.ds(r * BLK, BLK)
+        resid = acc_ref[rows, :] + x_ref[rows, :].astype(F32) + vec(4)
+        normed, inverse = norm(resid)
+        acc_ref[rows, :] = resid + vec(7)
+        n2_ref[rows, :] = normed.astype(BF16)
+        a2_ref[rows, :] = (normed * vec(5) + vec(6)).astype(BF16)
+        rs2_ref[rows, :] = jnp.broadcast_to(inverse, (BLK, 128))
+        add_vec(7, colsum(cot_ref[rows, :].astype(F32)))
+        g2_ref[rows, :] = jnp.zeros((BLK, D), F32)
+
+    loop(4, second_norm)
+
+    def feed(j):
+        up, down = 4 + j, 8 + j
+        bias = bup_ref[j, 0:1]
+
+        def part(r):
+            rows = pl.ds(r * 512, 512)
+            u = dot(a2_ref[rows, :], weight(up), 1, 0) + bias
+            back = dot(cot_ref[rows, :], weight(down), 1, 1)
+            square = u * u
+            th = jnp.tanh(u * (0.7978845608028654 + 0.035677408136300125 * square))
+            half = 0.5 + 0.5 * th
+            a3_ref[rows, :] = (u * half).astype(BF16)
+            slope = half + (half * (1.0 - th)) * (u * (0.7978845608028654 + 0.10703222440890037 * square))
+            gu = (back * slope).astype(BF16)
+            gu_ref[rows, :] = gu
+            bup_ref[j, 1:2] += colsum(gu.astype(F32))
+
+        loop(2, part)
+        acc_ref[...] += dot(a3_ref[...], weight(down), 1, 0)
+        g2_ref[...] += dot(gu_ref[...], weight(up), 1, 1)
+        w_ref[down] = dot(a3_ref[...], cot_ref[...], 0, 0).astype(BF16).reshape(4, 4, 48, D)
+        w_ref[up] = dot(a2_ref[...], gu_ref[...], 0, 0).astype(BF16).reshape(4, 4, 48, D)
+
+    for j in range(4):
+        bup_ref[j, 0:1] = vec(8 + j)
+        bup_ref[j, 1:2] = jnp.zeros((1, D), F32)
+    loop(4, feed)
+    for j in range(4):
+        vg_ref[8 + j : 9 + j, :] = bup_ref[j, 1:2]
+
+    def second_back(r):
+        rows = pl.ds(r * BLK, BLK)
+        a3_ref[rows, :] = acc_ref[rows, :].astype(BF16)
+        g2 = g2_ref[rows, :]
+        normed = n2_ref[rows, :].astype(F32)
+        add_vec(5, colsum(g2 * normed))
+        add_vec(6, colsum(g2))
+        t = g2 * vec(5)
+        first = jnp.mean(t, -1, keepdims=True)
+        second = jnp.mean(t * normed, -1, keepdims=True)
+        grad = cot_ref[rows, :].astype(F32) + rs2_ref[rows, 0:1] * (t - first - normed * second)
+        g2_ref[rows, :] = grad
+        lowered = grad.astype(BF16)
+        a2_ref[rows, :] = lowered
+        add_vec(4, colsum(lowered.astype(F32)))
+
+    loop(4, second_back)
+    out_copy = pltpu.make_async_copy(a3_ref, act_hbm, sem.at[0])
+    out_copy.start()
+    gu_ref[...] = dot(a2_ref[...], weight(3), 1, 1).astype(BF16)
+    w_ref[3] = dot(o_ref[...], a2_ref[...], 0, 0).astype(BF16).reshape(4, 4, 48, D)
+    loop(12, lambda i: attention_backward(i, (q_ref, k_ref, v_ref, gu_ref, p_ref), mine))
+
+    add_vec(2, colsum(q_ref[...].astype(F32)))
+    add_vec(3, colsum(v_ref[...].astype(F32)))
+    out_copy.wait()
+    g1e = dot(k_ref[1024:1536, :], weight(1), 1, 1) + dot(v_ref[1024:1536, :], weight(2), 1, 1)
+    a3_ref[0:512, :] = g1e.astype(BF16)
+    acc_ref[...] = dot(q_ref[...], weight(0), 1, 1)
+    acc_ref[...] += dot(k_ref[0:1024, :], weight(1), 1, 1)
+    acc_ref[...] += dot(v_ref[0:1024, :], weight(2), 1, 1)
+    w_ref[0] = dot(a1_ref[0:1024, :], q_ref[...], 0, 0).astype(BF16).reshape(4, 4, 48, D)
+    w_ref[1] = dot(a1_ref[...], k_ref[...], 0, 0).astype(BF16).reshape(4, 4, 48, D)
+    w_ref[2] = dot(a1_ref[...], v_ref[...], 0, 0).astype(BF16).reshape(4, 4, 48, D)
+
+    def extra_back(r):
+        rows = pl.ds(1024 + r * BLK, BLK)
+        normed, _ = norm(x_ref[rows, :].astype(F32))
+        g1 = a3_ref[pl.ds(r * BLK, BLK), :].astype(F32)
+        add_vec(0, colsum(g1 * normed))
+        add_vec(1, colsum(g1))
+
+    loop(2, extra_back)
+
+    def first_back(r):
+        rows = pl.ds(r * BLK, BLK)
+        normed, inverse = norm(x_ref[rows, :].astype(F32))
+        g1 = acc_ref[rows, :]
+        add_vec(0, colsum(g1 * normed))
+        add_vec(1, colsum(g1))
+
+    loop(4, first_back)
+    pairs = ((acc_ref, g1_hbm), (g2_ref, gr_hbm), (a3_ref.at[0:512], g1e_hbm), (w_ref, g_hbm), (vg_ref, vg_hbm))
+    for i, (src, dst) in enumerate(pairs):
+        pltpu.make_async_copy(src, dst, sem.at[i]).start()
+    for i, (src, dst) in enumerate(pairs):
+        pltpu.make_async_copy(src, dst, sem.at[i]).wait()
+
+
+def fast_device(
+    layer_input, segments, ln1_gain, ln1_bias, w_qkv, q_bias, v_bias, w_attn_out, b_attn_out,
+    ln2_gain, ln2_bias, w_up, b_up, w_down, b_down, cotangent,
+):
+    mine = lax.axis_index("ctx")
+    x = layer_input.reshape(1024, D)
+    cot = cotangent.reshape(1024, D)
+    seg = segments.reshape(2, 1024)
+    own = lax.dynamic_slice_in_dim(x.reshape(2, 512, D), mine * BLK, BLK, 1)
+    extra = lax.ppermute(own, "ctx", ((0, 1), (1, 0))).reshape(512, D)
+
+    def gather(v):
+        return lax.all_gather(v, "fsdp", axis=0, tiled=True)
+
+    qkv, up = gather(w_qkv), gather(w_up)
+    blocks = [qkv[:, D * i : D * i + D] for i in range(3)] + [gather(w_attn_out)]
+    blocks += [up[:, D * i : D * i + D] for i in range(4)]
+    w = jnp.concatenate([jnp.stack(blocks), gather(w_down).reshape(4, D, D)]).reshape(12, 4, 4, 48, D)
+    rows = [ln1_gain, ln1_bias, q_bias, v_bias, b_attn_out, ln2_gain, ln2_bias, b_down]
+    vec = jnp.concatenate(
+        [jnp.stack([gather(v) for v in rows]), gather(b_up).reshape(4, D), jnp.zeros((4, D), BF16)]
+    )
+    big = lambda *shape, dtype=BF16: jax.ShapeDtypeStruct(shape, dtype)
+    hbm = pl.BlockSpec(memory_space=pltpu.HBM)
+    vmem = pl.BlockSpec(memory_space=pltpu.VMEM)
+    act, g1, gr, g1e, g, vg = pl.pallas_call(
+        layer_kernel,
+        out_shape=(
+            big(1024, D), big(1024, D, dtype=F32), big(1024, D, dtype=F32), big(512, D),
+            big(12, 4, 4, 48, D), big(16, D, dtype=F32),
+        ),
+        in_specs=[hbm, hbm, hbm, vmem, hbm, vmem],
+        out_specs=(hbm,) * 6,
+        scratch_shapes=[
+            pltpu.VMEM((12, 4, 4, 48, D), BF16),
+            pltpu.VMEM((1536, D), BF16),
+            pltpu.VMEM((1024, D), BF16),
+            pltpu.VMEM((1024, D), BF16),
+            pltpu.VMEM((1536, D), BF16),
+            pltpu.VMEM((1536, D), BF16),
+            pltpu.VMEM((1024, D), BF16),
+            pltpu.VMEM((12, 2, 3 * BLK, BLK), BF16),
+            pltpu.VMEM((2, 3 * BLK, BLK), F32),
+            pltpu.VMEM((1024, D), F32),
+            pltpu.VMEM((1024, D), BF16),
+            pltpu.VMEM((1024, D), BF16),
+            pltpu.VMEM((1024, 128), F32),
+            pltpu.VMEM((1024, D), F32),
+            pltpu.VMEM((1536, D), BF16),
+            pltpu.VMEM((1024, D), BF16),
+            pltpu.VMEM((1024, D), BF16),
+            pltpu.VMEM((16, D), F32),
+            pltpu.VMEM((4, 8, D), F32),
+            pltpu.SemaphoreType.DMA((8,)),
+        ],
+        compiler_params=pltpu.CompilerParams(vmem_limit_bytes=63_000_000),
+        name="layer",
+    )(x, extra, cot, seg, w, vec)
+    back = lax.ppermute(g1e.astype(F32), "ctx", ((0, 1), (1, 0))).reshape(2, BLK, D)
+    g1 = g1.reshape(2, 512, D)
+    mid = lax.dynamic_slice_in_dim(g1, mine * BLK, BLK, 1) + back
+    g1 = lax.dynamic_update_slice_in_dim(g1, mid, mine * BLK, 1).reshape(1024, D)
+    normed, inverse = normalize_parts(x.astype(F32))
+    gx = (gr + normalize_back(g1 * vec[0].astype(F32), normed, inverse)).astype(BF16)
+    g = g.astype(F32).reshape(12, D, D)
+
+    def scatter(v):
+        return lax.psum(lax.psum_scatter(v, "fsdp", scatter_dimension=0, tiled=True), "ctx")
+
+    g_qkv = scatter(jnp.concatenate([g[0], g[1], g[2]], 1))
+    g_out = scatter(g[3])
+    g_up = scatter(jnp.concatenate([g[4], g[5], g[6], g[7]], 1))
+    g_down = scatter(g[8:].reshape(4 * D, D))
+    sums = lax.psum(vg, ("ctx", "fsdp"))
+    f = lax.axis_index("fsdp")
+    part = lambda i: lax.dynamic_slice_in_dim(sums[i], f * 48, 48)
+    g_bup = lax.dynamic_slice_in_dim(sums[8:12].reshape(4 * D), f * 192, 192)
+    return (
+        act.reshape(2, 1, 512, D), gx.reshape(2, 1, 512, D), part(0), part(1), g_qkv, part(2), part(3),
+        g_out, part(4), part(5), part(6), g_up, g_bup, g_down, part(7),
+    )
+
+
 def solution(mesh):
     in_specs = (
         P(None, "fsdp", "ctx", None),
@@ -442,6 +818,7 @@
         P("fsdp", None),
         P("fsdp"),
     )
+    fast = mesh.shape["ctx"] == 2 and mesh.shape["fsdp"] == 16
     return jax.shard_map(
-        on_device, mesh=mesh, in_specs=in_specs, out_specs=out_specs, check_vma=False
-    )
+        fast_device if fast else on_device, mesh=mesh, in_specs=in_specs, out_specs=out_specs, check_vma=False
+    )

time: 1300 us -> 796 us (0.61); the launches traced: 1280 us -> 787 us
  local copies, waits for them, and re-layouts: 353 us -> 60.4 us
  matrix products: 259 us -> 0 us
  Pallas kernels: 0 us -> 105 us
  other arithmetic: 53.1 us -> 23.9 us
    dot_general x60 -> x0, matrix products: 259 us -> none  [the longest x4 28.5 us: compute(): jnp.einsum('hqk,khd->qhd', lowered, values_tile, preferred_element_type=j...]
    dynamic_update_slice x16 -> x0, local copies, waits for them, and re-layouts: 252 us -> none  [attention_back(): lax.scan(advance, jnp.zeros(query.shape, jnp.float32), tiles)]
    pallas_call x0 -> x1, Pallas kernels: none -> 105 us  [fast_device(): pl.pallas_call(layer_kernel, out_shape=(big(1024, D), big(1024, D, dtype=...]
    reduce_scatter x6 -> x4, waiting for transfers between devices: 387 us -> 294 us  [scatter(): lax.psum_scatter(v, 'fsdp', scatter_dimension=0, tiled=True)]
    unnamed x2 -> x1, blocking collectives: 123 us -> 61.7 us
    psum x1, blocking collectives: 5.55 us -> 67 us  [fast_device(): sums = lax.psum(vg, ('ctx', 'fsdp'))]
    psum x1, waiting for transfers between devices: 0.01 us -> 46.7 us  [scatter(): lax.psum(lax.psum_scatter(v, 'fsdp', scatter_dimension=0, tiled=True), 'c...]
    all_gather x6 -> x4, waiting for transfers between devices: 71.5 us -> 105 us  [gather(): return lax.all_gather(v, 'fsdp', axis=0, tiled=True)]
  transfers between devices with their start and end apart: 13 -> 11, of which waited for: 8 -> 7; matrix products, arithmetic and copies ran while one was open for 33% -> 9% of each run, Pallas kernels for 0% -> 0%
where the time goes in v1:
time: 796 us; the launch traced here: 787 us
  waiting for transfers between devices  449 us (56%)
  blocking collectives  129 us (16%)
  Pallas kernels  105 us (13%)
  local copies, waits for them, and re-layouts  60.4 us (8%)
  other arithmetic  23.9 us (3%)
  between operations  15.8 us (2%)
    reduce_scatter x4, waiting for transfers between devices, scatter(): lax.psum_scatter(v, 'fsdp', scatter_dimension=0, tiled=True)  294 us
    all_gather x4, waiting for transfers between devices, gather(): return lax.all_gather(v, 'fsdp', axis=0, tiled=True)  105 us
    pallas_call x1, Pallas kernels, fast_device(): pl.pallas_call(layer_kernel, out_shape=(big(1024, D), big(1024, D, dtype=...  105 us
    psum x1, blocking collectives, fast_device(): sums = lax.psum(vg, ('ctx', 'fsdp'))  67 us
    unnamed x1, blocking collectives  61.7 us
    psum x1, waiting for transfers between devices, scatter(): lax.psum(lax.psum_scatter(v, 'fsdp', scatter_dimension=0, tiled=True), 'c...  46.7 us
    unnamed x48, local copies, waits for them, and re-layouts  29.4 us
  transfers between devices with their start and end apart: 11, of which 7 were waited for; matrix products, arithmetic and copies ran while one was open for 9% of the time, Pallas kernels for 0%

profile of v1, /device:TPU:0, one launch (start us, length us, event | category | flops | bytes accessed | tf_op | source)
XLA Modules:
  0.0 787.0 jit_solution(6172068227359117556)
XLA Ops:
  7.2 0.7 all-gather.5.cloned.1.call-update
  8.0 0.7 all-gather.7.cloned.1.call-update
  8.7 0.7 all-gather.9.cloned.1.call-update
  9.4 0.5 all-gather.11.cloned.1.call-update
  10.0 1.2 dynamic-slice_bitcast_fusion
  11.2 3.0 collective-permute-start
  14.2 1.2 dynamic-slice.9
  16.8 0.8 dynamic-update-slice.6
  17.6 0.8 dynamic-update-slice.5
  18.5 0.8 dynamic-update-slice.4
  19.3 0.8 dynamic-update-slice.3
  20.1 0.8 dynamic-update-slice.2
  21.0 0.8 dynamic-update-slice.1
  21.8 0.8 dynamic-update-slice
  22.6 0.8 dynamic-update-slice.7
  23.5 0.8 dynamic-update-slice.8
  24.3 61.7 %all-reduce.10 = (bf16[768]{0:T(1024)(128)(2,1)S(1)}, bf16[768]{0:T(1024)(128)(2,1)S(1)}, bf16[768]{0:T(1024)(128)(2,1)S(1)}, bf16[768]{0:T(1024)(128)(2,1)S(1)}...) all-reduce(bf16[768]{0:T(1024)(128)(2,1)S(1)} %dynamic-update-slice, ...), channel_id=1, replica_groups=mesh['ctx'=2,'fsdp'=16] {'fsdp'}, use_global_device_ids=true, to_apply=%add | all-reduce | flops 9216 | bytes 36864
  86.1 1.3 copy.39
  87.4 1.3 concatenate.41.vec_ref
  88.7 2.2 fusion.23
  90.9 1.1 constant_dynamic-update-slice_fusion.8
  92.0 1.1 constant_dynamic-update-slice_fusion.7
  93.1 1.1 constant_dynamic-update-slice_fusion.6
  94.2 6.0 all-gather.7.cloned.1.call-done
  100.2 2.4 constant_dynamic-update-slice_fusion.5
  102.6 52.3 %all-gather.9.cloned.1.call-done = bf16[768,3072]{1,0:T(8,128)(2,1)} async-done(((bf16[48,3072]{1,0:T(8,128)(2,1)}), bf16[768,3072]{1,0:T(8,128)(2,1)}) %all-gather.9.cloned.1.call-update) | async-done | bytes 4718608 | tf_op jit(solution)/shard_map/all_gather | solution.py:714
  154.9 2.7 fusion.22
  157.6 1.1 constant_dynamic-update-slice_fusion.4
  158.7 1.1 constant_dynamic-update-slice_fusion.3
  159.8 1.1 constant_dynamic-update-slice_fusion.2
  160.9 1.1 constant_dynamic-update-slice_fusion.1
  162.0 47.0 %all-gather.11.cloned.1.call-done = bf16[3072,768]{1,0:T(8,128)(2,1)} async-done(((bf16[192,768]{1,0:T(8,128)(2,1)}), bf16[3072,768]{1,0:T(8,128)(2,1)}) %all-gather.11.cloned.1.call-update) | async-done | bytes 4718608 | tf_op jit(solution)/shard_map/all_gather | solution.py:714
  209.0 5.0 constant_dynamic-update-slice_fusion.w_hbm
  214.0 0.9 copy-done.3
  214.9 104.8 %layer.1 = (bf16[1024,768]{1,0:T(8,128)(2,1)}, f32[1024,768]{1,0:T(8,128)}, f32[1024,768]{1,0:T(8,128)}, bf16[512,768]{1,0:T(8,128)(2,1)}, bf16[12,4,4,48,768]{4,3,2,1,0:T(8,128)(2,1)}, /*index=5*/f32[16,768]{1,0:T(8,128)}) custom-call(bf16[1024,768]{1,0:T(8,128)(2,1)} %bitcast.87, bf16[512,768]{1,0:T(8,128)(2,1)} %bitcast.110, bf16[1024,768]{1,0:T(8,128)(2,1)} %bitcast.106, ...), custom_call_target="tpu_custom_call" | custom-call | tf_op jit(solution)/shard_map/layer/pallas_call | solution.py:727
  319.7 8.2 %fusion.21 = (f32[1,4,4,48,768]{4,3,2,1,0:T(8,128)S(1)}, f32[1,4,4,48,768]{4,3,2,1,0:T(8,128)}, f32[1,4,4,48,768]{4,3,2,1,0:T(8,128)}, f32[1,4,4,48,768]{4,3,2,1...) fusion(bf16[12,4,4,48,768]{4,3,2,1,0:T(8,128)(2,1)} %get-tuple-, ...), kind=kLoop, calls=%fused_computation.52 | loop fusion | bytes 37748736 | tf_op jit(solution)/shard_map/slice | solution.py:773
  327.9 0.0 reduce-scatter.5.cloned.1.call-start
  328.0 5.2 pad_maximum_fusion.1
  333.2 0.0 reduce-scatter.11.cloned.1.call-start
  333.3 7.4 slice.132
  340.7 0.0 reduce-scatter.9.cloned.1.call-start
  340.7 7.7 pad_maximum_fusion
  348.5 1.0 copy-done.4
  349.5 1.3 convert_element_type.26
  350.8 1.5 collective-permute-start.1
  352.3 0.3 convert_reduce_fusion
  352.6 0.6 fusion.1
  353.2 67.0 %psum.35 = f32[16,768]{1,0:T(8,128)S(1)} all-reduce(f32[16,768]{1,0:T(8,128)S(1)} %copy-done.5), channel_id=1, replica_groups=mesh['ctx'=2,'fsdp'=16] {'ctx','fsdp'}, use_global_device_ids=true, to_apply=%region_4.0 | all-reduce | flops 12288 | bytes 98304 | tf_op jit(solution)/shard_map/psum | solution.py:775
  420.3 63.1 %reduce-scatter.5.cloned.1.call-done = f32[48,2304]{1,0:T(8,128)} async-done(((f32[768,2304]{1,0:T(8,128)}), f32[48,2304]{1,0:T(8,128)}) %reduce-scatter.5.cloned.1.call-update) | async-done | bytes 442384 | tf_op jit(solution)/shard_map/reduce_scatter | solution.py:769
  483.4 115.0 %reduce-scatter.11.cloned.1.call-done = f32[192,768]{1,0:T(8,128)} async-done(((f32[3072,768]{1,0:T(8,128)}), f32[192,768]{1,0:T(8,128)}) %reduce-scatter.11.cloned.1.call-update) | async-done | bytes 589840 | tf_op jit(solution)/shard_map/reduce_scatter | solution.py:769
  598.4 115.8 %reduce-scatter.9.cloned.1.call-done = f32[48,3072]{1,0:T(8,128)} async-done(((f32[768,3072]{1,0:T(8,128)}), f32[48,3072]{1,0:T(8,128)}) %reduce-scatter.9.cloned.1.call-update) | async-done | bytes 589840 | tf_op jit(solution)/shard_map/reduce_scatter | solution.py:769
  714.2 0.6 fusion.11
  714.8 0.6 dynamic_slice.68
  715.4 0.6 fusion.17
  716.0 0.6 fusion.15
  716.6 0.6 fusion.13
  717.2 2.9 add_dynamic-update-slice_fusion
  720.1 3.4 multiply_reduce_fusion
  723.6 2.5 fusion.10
  726.1 46.7 %all-reduce.13.cloned.1.call-done = (f32[48,2304]{1,0:T(8,128)}, f32[48,768]{1,0:T(8,128)}, f32[48,3072]{1,0:T(8,128)}, f32[192,768]{1,0:T(8,128)}) async-done(((f32[48,2304]{1,0:T(8,128)}, f32[48,768]{1,0:T(8,128)}, f32[48,3072]{1,0:T(8,128)}, f32[192,768]{1,0:T(8,128)}), (f32[48,2304]{1,0:T(8,128)}, f32[48,768]{1,0:T(8,128)}, f32[48,3072]{1,0:T(8,128)}, ...) | async-done | bytes 1769488 | tf_op jit(solution)/shard_map/psum | solution.py:769
  772.8 1.8 copy.62
  774.6 1.6 copy.63
  776.2 1.9 copy.64
  778.1 1.9 copy.65
  (55 shorter events, 0.5 us)
Async XLA Ops:
  7.2 81.5 %all-gather.5.cloned.1.call-start = ((), (), s32[]{:S(2)}) async-start(), calls=%async_computation.4 | async-start | bytes 3760128 | tf_op jit(solution)/shard_map/all_gather | solution.py:714
  7.9 92.3 %all-gather.7.cloned.1.call-start = ((), (), s32[]{:S(2)}) async-start(), calls=%async_computation.5 | async-start | bytes 1253376 | tf_op jit(solution)/shard_map/all_gather | solution.py:714
  8.7 146.3 %all-gather.9.cloned.1.call-start = ((), (), s32[]{:S(2)}) async-start(), calls=%async_computation.6 | async-start | bytes 5013504 | tf_op jit(solution)/shard_map/all_gather | solution.py:714
  9.4 199.6 %all-gather.11.cloned.1.call-start = ((), (), s32[]{:S(2)}) async-start(), calls=%async_computation.7 | async-start | bytes 5013504 | tf_op jit(solution)/shard_map/all_gather | solution.py:714
  10.0 410.3 %reduce-scatter.7.cloned.1.call-start = ((), (), s32[]{:S(2)}) async-start(), calls=%async_computation.9 | async-start | bytes 2506752 | tf_op jit(solution)/shard_map/reduce_scatter | solution.py:769
  11.2 202.8 %collective-permute-start = (bf16[2,256,768]{2,1,0:T(8,128)(2,1)S(1)}, bf16[2,256,768]{2,1,0:T(8,128)(2,1)S(1)}, u32[]{:S(2)}, u32[]{:S(2)}) collective-permute-start(bf16[2,256,768]{2,1,0:T(8,128)(2,1)S(1)} %dynamic-slice_bitcast_fusion), channel_id=1, source_target_pairs={{0,16},{16,0},{1,17},{17,1},{2,18},{18,2},{3,19},{19,3},{4,20},{20... | collective-permute-start | bytes 2359304 | tf_op jit(solution)/shard_map/ppermute | solution.py:711
  214.0 0.9 copy-start.3
  327.9 155.5 %reduce-scatter.5.cloned.1.call-start = ((), (), s32[]{:S(2)}) async-start(), calls=%async_computation.8 | async-start | bytes 7520256 | tf_op jit(solution)/shard_map/reduce_scatter | solution.py:769
  333.2 265.2 %reduce-scatter.11.cloned.1.call-start = ((), (), s32[]{:S(2)}) async-start(), calls=%async_computation.11 | async-start | bytes 10027008 | tf_op jit(solution)/shard_map/reduce_scatter | solution.py:769
  340.7 373.5 %reduce-scatter.9.cloned.1.call-start = ((), (), s32[]{:S(2)}) async-start(), calls=%async_computation.10 | async-start | bytes 10027008 | tf_op jit(solution)/shard_map/reduce_scatter | solution.py:769
  348.4 1.1 copy-start.4
  348.4 3.8 copy-start
  348.4 4.8 copy-start.5
  348.5 424.3 %all-reduce.13.cloned.1.call-start = ((), (), s32[]{:S(2)}) async-start(), calls=%async_computation.12 | async-start | bytes 3538944 | tf_op jit(solution)/shard_map/psum | solution.py:769
  350.8 366.4 %collective-permute-start.1 = (f32[512,768]{1,0:T(8,128)}, f32[512,768]{1,0:T(8,128)S(1)}, u32[]{:S(2)}, u32[]{:S(2)}) collective-permute-start(f32[512,768]{1,0:T(8,128)} %convert_element_type.26), channel_id=1, source_target_pairs={{0,16},{16,0},{1,17},{17,1},{2,18},{18,2},{3,19},{19,3},{4,20},{20... | collective-permute-start | bytes 4718600 | tf_op jit(solution)/shard_map/ppermute | solution.py:760
  717.2 6.3 copy-start.2
  720.1 3.5 copy-start.1
Sparse Core Ops, SparseCore 0:
  10.3 50.2 all-gather.4
  62.9 37.2 all-gather.6
  102.5 52.3 all-gather.8
  157.1 51.9 all-gather.10
  328.0 61.8 reduce-scatter.6
  394.3 89.0 reduce-scatter.4
  487.5 110.8 reduce-scatter.10
  603.0 111.0 reduce-scatter.8
  716.7 56.0 all-reduce.12

commit v2 on v1

--- a/solution.py
+++ b/solution.py
@@ -457,9 +457,10 @@
         solo = row(mine * 2 * BLK + mine * BLK)
         wide = row(mine * 2 * BLK + (1 - mine) * BLK)
         extra = row((1 - mine) * 3 * BLK)
-        bias_ref[micro, 0:BLK] = jnp.where((solo.T == solo) & causal, 0.0, NEG)
-        bias_ref[micro, BLK : 2 * BLK] = jnp.where(extra.T == wide, 0.0, NEG)
-        bias_ref[micro, 2 * BLK :] = jnp.where((wide.T == wide) & causal, 0.0, NEG)
+        rows = slice(micro * BLK, micro * BLK + BLK)
+        tiles = ((solo.T == solo) & causal, extra.T == wide, (wide.T == wide) & causal)
+        for t, allowed in enumerate(tiles):
+            bias_ref[rows, t * BLK : t * BLK + BLK] = jnp.where(allowed, 0.0, NEG).astype(BF16)
 
 
 def attention_rows(micro, mine):
@@ -496,13 +497,18 @@
     vt_s, vt_x, vt_e = v_ref[solo, pair].T, v_ref[wide, pair].T, v_ref[extra, pair].T
     q_s, q_x = halves(q_ref[solo, pair]), halves(q_ref[wide, pair])
     outs_s, outs_x = [], []
+
+    def bias(t):
+        rows = pl.ds(pl.multiple_of(micro * BLK, BLK), BLK)
+        return bias_ref[rows, t * BLK : t * BLK + BLK].astype(F32)
+
     for head in range(2):
         rows = slice(head * HD, head * HD + HD)
-        (p_s,) = softmax_columns([dot(k_s, q_s[head], 1, 1) + bias_ref[micro, 0:BLK]])
+        (p_s,) = softmax_columns([dot(k_s, q_s[head], 1, 1) + bias(0)])
         p_e, p_x = softmax_columns(
             [
-                dot(k_e, q_x[head], 1, 1) + bias_ref[micro, BLK : 2 * BLK],
-                dot(k_x, q_x[head], 1, 1) + bias_ref[micro, 2 * BLK :],
+                dot(k_e, q_x[head], 1, 1) + bias(1),
+                dot(k_x, q_x[head], 1, 1) + bias(2),
             ]
         )
         p_ref[index, head, 0:BLK] = p_s
@@ -557,45 +563,497 @@
     q_ref[wide, pair] = (jnp.concatenate(outs_x, 0).T * 0.125).astype(BF16)
 
 
+MESH = pl.DeviceIdType.MESH
+HALF = D // 2
+
+
+class Place:
+    def __init__(self):
+        self.c = lax.axis_index("ctx")
+        f = lax.axis_index("fsdp")
+        self.z, self.y, self.k = f // 4, (f // 2) % 2, f % 2
+        self.sibling = self.at(self.c, self.z, self.y, 1 - self.k)
+        self.beside = self.at(1 - self.c, self.z, self.y, self.k)
+        self.across = self.at(self.c, self.z, 1 - self.y, self.k)
+
+    def at(self, c, z, y, k):
+        return (c, z * 4 + y * 2 + k)
+
+    def level(self, step):
+        return lax.rem(self.z + step, 4)
+
+    def along(self, step):
+        return self.at(self.c, self.level(step), self.y, self.k)
+
+    def pick(self, first, second):
+        return first + self.k * (second - first)
+
+    def turn(self, core):
+        side = self.k if core == 0 else 1 - self.k
+        c = self.c + (1 - side) * (1 - 2 * self.c)
+        y = self.y + side * (1 - 2 * self.y)
+        return self.at(c, self.z, y, self.k)
+
+
+def half(index):
+    return pl.ds(pl.multiple_of(index * HALF, 128), HALF)
+
+
+def send(source, target, sends, recvs, device):
+    return pltpu.make_async_remote_copy(
+        src_ref=source, dst_ref=target, send_sem=sends, recv_sem=recvs, device_id=device, device_id_type=MESH
+    )
+
+
+def begin(copies):
+    for copy in copies:
+        copy.start()
+
+
+def landed(copies):
+    for copy in copies:
+        copy.wait_recv()
+
+
+def gone(copies):
+    for copy in copies:
+        copy.wait_send()
+
+
+class Gather:
+    def __init__(self, place, sources, w_ref, d_ref, vec_ref, sends, recvs, local):
+        self.p, self.sources = place, sources
+        self.w, self.d, self.v = w_ref, d_ref, vec_ref
+        self.sends, self.recvs, self.local = sends, recvs, local
+
+    def whole(self, piece):
+        return self.v if piece is None else self.w.at[piece]
+
+    def row(self, piece):
+        return 12 if piece is None else piece
+
+    def own(self, piece):
+        if piece is None:
+            return self.sources[3]
+        if piece < 3:
+            return self.sources[0].at[:, piece * D : piece * D + D]
+        if piece == 3:
+            return self.sources[1]
+        return self.sources[2].at[:, (piece - 4) * D : (piece - 3) * D]
+
+    def own_half(self, piece):
+        cols = half(self.p.c)
+        if piece is None:
+            return self.sources[3].at[:, cols]
+        if piece == 3:
+            return self.sources[1].at[:, cols]
+        base, first = (self.sources[0], 0) if piece < 3 else (self.sources[2], 4)
+        return base.at[:, pl.ds(pl.multiple_of((piece - first) * D + self.p.c * HALF, 128), HALF)]
+
+    def keep(self, piece):
+        p = self.p
+        return pltpu.make_async_copy(
+            self.own(piece), self.whole(piece).at[p.z, p.y, p.k], self.local.at[self.row(piece)]
+        )
+
+    def keep_down(self):
+        p = self.p
+        return pltpu.make_async_copy(self.sources[4], self.d.at[p.z, p.y, p.k], self.local.at[8])
+
+    def z_copy(self, piece, step, level):
+        p, row = self.p, self.row(piece)
+        return send(
+            self.own_half(piece),
+            self.whole(piece).at[level, p.y, p.k, :, half(p.c)],
+            self.sends.at[row, step - 1],
+            self.recvs.at[row, step - 1],
+            p.along(step),
+        )
+
+    def z_down(self, step, level, sem):
+        p = self.p
+        return send(
+            self.sources[4].at[:, half(p.c)],
+            self.d.at[level, p.y, p.k, :, half(p.c)],
+            self.sends.at[13, sem],
+            self.recvs.at[13, sem],
+            p.along(step),
+        )
+
+    def start(self, pieces):
+        for piece in pieces:
+            self.keep(piece).start()
+            for step in (1, 2, 3):
+                self.z_copy(piece, step, self.p.z).start()
+
+    def start_down(self):
+        self.keep_down().start()
+        for step in (1, 2, 3):
+            self.z_down(step, self.p.z, step - 1).start()
+
+    def copies(self, piece):
+        p, row = self.p, self.row(piece)
+        whole = self.whole(piece)
+
+        def to(part, column, device):
+            return send(part, part, self.sends.at[row, column], self.recvs.at[row, column], device)
+
+        def beside():
+            return [
+                to(whole.at[p.level(step), p.y, p.k, :, half(p.c)], 2 + step, p.beside) for step in (1, 2, 3)
+            ]
+
+        def across():
+            return [to(whole.at[:, p.y, p.k, :, half(p.c)], 6, p.across)]
+
+        def forward():
+            part = whole.at[:, p.pick(1 - p.y, p.y), p.k, :, half(p.pick(p.c, 1 - p.c))]
+            return [to(part, 7, p.turn(0))]
+
+        def sibling():
+            return [to(whole.at[:, :, p.k], 8, p.sibling)]
+
+        return beside, across, forward, sibling
+
+    def copies_down(self, j):
+        p, row = self.p, 8 + j
+
+        def to(part, column, device):
+            return send(part, part, self.sends.at[row, column], self.recvs.at[row, column], device)
+
+        def beside():
+            return [to(self.d.at[j, p.y, p.k, :, half(p.c)], 3, p.beside)]
+
+        def across():
+            return [to(self.d.at[j, p.y, p.k, :, half(p.c)], 6, p.across)]
+
+        def forward():
+            part = self.d.at[j, p.pick(1 - p.y, p.y), p.k, :, half(p.pick(p.c, 1 - p.c))]
+            return [to(part, 7, p.turn(0))]
+
+        def sibling():
+            return [to(self.d.at[j, :, p.k], 8, p.sibling)]
+
+        return beside, across, forward, sibling
+
+    def stage(self, number, piece):
+        if isinstance(piece, tuple):
+            return self.stage_down(number, piece[1])
+        beside, across, forward, sibling = self.copies(piece)
+        if number == 2:
+            self.keep_wait(piece)
+            for step in (1, 2, 3):
+                self.z_wait(piece, step)
+            begin(beside() + across())
+        elif number == 3:
+            landed(beside() + across())
+            begin(forward())
+        elif number == 4:
+            landed(forward())
+            begin(sibling())
+        elif number == 5:
+            landed(sibling())
+        else:
+            gone(beside() + across() + forward() + sibling())
+
+    def keep_wait(self, piece):
+        p = self.p
+        part = self.whole(piece).at[p.z, p.y, p.k]
+        pltpu.make_async_copy(part, part, self.local.at[self.row(piece)]).wait()
+
+    def z_wait(self, piece, step):
+        p, row = self.p, self.row(piece)
+        part = self.whole(piece).at[p.level(4 - step), p.y, p.k, :, half(p.c)]
+        send(part, part, self.sends.at[row, step - 1], self.recvs.at[row, step - 1], p.along(step)).wait_recv()
+
+    def stage_down(self, number, j):
+        p = self.p
+        beside, across, forward, sibling = self.copies_down(j)
+        away = p.z != j
+        if number == 2:
+
+            @pl.when(away)
+            def _():
+                step = lax.rem(p.z - j + 4, 4)
+                part = self.d.at[j, p.y, p.k, :, half(p.c)]
+                landed([send(part, part, self.sends.at[13, step - 1], self.recvs.at[13, step - 1], p.along(1))])
+                begin(beside())
+
+            @pl.when(p.z == j)
+            def _():
+                self.keep_down().wait()
+
+            begin(across())
+        elif number == 3:
+
+            @pl.when(away)
+            def _():
+                landed(beside())
+
+            landed(across())
+            begin(forward())
+        elif number == 4:
+            landed(forward())
+            begin(sibling())
+        elif number == 5:
+            landed(sibling())
+        else:
+
+            @pl.when(away)
+            def _():
+                gone(beside())
+
+            gone(across() + forward() + sibling())
+
+    def finish(self):
+        for piece in (None, *range(8)):
+            for step in (1, 2, 3):
+                self.z_copy(piece, step, self.p.z).wait_send()
+        for step in (1, 2, 3):
+            self.z_down(step, self.p.z, step - 1).wait_send()
+
+
+class Scatter:
+    def __init__(self, place, w_ref, d_ref, rings, fin_ref, find_ref, sends, recvs):
+        self.p, self.w, self.d = place, w_ref, d_ref
+        self.rings, self.fin, self.find = rings, fin_ref, find_ref
+        self.sends, self.recvs = sends, recvs
+
+    def part(self, block, y, col):
+        if isinstance(block, tuple):
+            return self.d.at[block[1], y, self.p.k, :, half(col)]
+        return self.w.at[block, :, y, self.p.k, :, half(col)]
+
+    def row(self, block):
+        return 8 + block[1] if isinstance(block, tuple) else block
+
+    def ring(self, block, which, slot):
+        return self.rings[2 * which + (1 if isinstance(block, tuple) else 0)].at[slot]
+
+    def sem(self, block, column):
+        row = self.row(block)
+        return self.sends.at[row, column], self.recvs.at[row, column]
+
+    def to_sibling(self, block, slot):
+        p = self.p
+        part = self.d.at[block[1], :, 1 - p.k] if isinstance(block, tuple) else self.w.at[block, :, :, 1 - p.k]
+        return send(part, self.ring(block, 0, slot), *self.sem(block, 0), p.sibling)
+
+    def first(self, block, slot, i):
+        p = self.p
+        part = self.part(block, p.pick(i, 1 - p.y), p.pick(1 - p.c, i))
+        ring = self.ring(block, 1, slot)
+        ring = ring.at[i] if isinstance(block, tuple) else ring.at[:, i]
+        return send(part, ring, *self.sem(block, 1 + i), p.turn(0))
+
+    def second(self, block, slot):
+        p = self.p
+        part = self.part(block, p.pick(1 - p.y, p.y), p.pick(p.c, 1 - p.c))
+        return send(part, self.ring(block, 2, slot), *self.sem(block, 3), p.turn(1))
+
+    def third(self, block, slot, step):
+        p = self.p
+        part = self.w.at[block, p.level(step), p.y, p.k, :, half(p.c)]
+        return send(part, self.rings[6].at[slot, step - 1], *self.sem(block, 3 + step), p.along(step))
+
+    def third_down(self, j, step):
+        p = self.p
+        part = self.part(("d", j), p.y, p.c)
+        return send(part, self.rings[7].at[step - 1], *self.sem(("d", j), 3 + step), p.at(p.c, j, p.y, p.k))
+
+    def last(self, block):
+        p = self.p
+        part = self.find.at[:, half(p.c)] if isinstance(block, tuple) else self.fin.at[block, :, half(p.c)]
+        return send(part, part, *self.sem(block, 7), p.beside)
+
+    def stage(self, number, block, slot):
+        p = self.p
+        down = isinstance(block, tuple)
+        if number == 0:
+            self.to_sibling(block, slot).start()
+        elif number == 1:
+            self.to_sibling(block, slot).wait_recv()
+            mine = self.d.at[block[1], :, p.k] if down else self.w.at[block, :, :, p.k]
+            mine[...] = mine[...] + self.ring(block, 0, slot)[...]
+            for i in (0, 1):
+                self.first(block, slot, i).start()
+        elif number == 2:
+            for i in (0, 1):
+                self.first(block, slot, i).wait_recv()
+                mine = self.part(block, p.pick(i, p.y), p.pick(p.c, i))
+                ring = self.ring(block, 1, slot)
+                mine[...] = mine[...] + (ring[i] if down else ring[:, i])
+            self.second(block, slot).start()
+        elif number == 3:
+            self.second(block, slot).wait_recv()
+            mine = self.part(block, p.y, p.c)
+            mine[...] = mine[...] + self.ring(block, 2, slot)[...]
+            if down:
+                j = block[1]
+
+                @pl.when(p.z != j)
+                def _():
+                    step = lax.rem(j - p.z + 4, 4)
+                    self.third_down(j, step).start()
+            else:
+                for step in (1, 2, 3):
+                    self.third(block, slot, step).start()
+        elif number == 4:
+            if down:
+                j = block[1]
+
+                @pl.when(p.z == j)
+                def _():
+                    total = self.part(block, p.y, p.c)[...].astype(F32)
+                    for step in (1, 2, 3):
+                        self.third_down(j, step).wait_recv()
+                        total = total + self.rings[7][step - 1].astype(F32)
+                    self.find[:, half(p.c)] = total.astype(BF16)
+                    self.last(block).start()
+            else:
+                total = self.w[block, p.z, p.y, p.k, :, half(p.c)].astype(F32)
+                for step in (1, 2, 3):
+                    self.third(block, slot, step).wait_recv()
+                    total = total + self.rings[6][slot, step - 1].astype(F32)
+                self.fin[block, :, half(p.c)] = total.astype(BF16)
+                self.last(block).start()
+        elif number == 5:
+            if down:
+
+                @pl.when(p.z == block[1])
+                def _():
+                    self.last(block).wait_recv()
+            else:
+                self.last(block).wait_recv()
+
+    def finish(self, block, slot):
+        p = self.p
+        self.to_sibling(block, slot).wait_send()
+        for i in (0, 1):
+            self.first(block, slot, i).wait_send()
+        self.second(block, slot).wait_send()
+        if isinstance(block, tuple):
+            j = block[1]
+
+            @pl.when(p.z != j)
+            def _():
+                self.third_down(j, lax.rem(j - p.z + 4, 4)).wait_send()
+
+            @pl.when(p.z == j)
+            def _():
+                self.last(block).wait_send()
+        else:
+            for step in (1, 2, 3):
+                self.third(block, slot, step).wait_send()
+            self.last(block).wait_send()
+
+
 def layer_kernel(
-    x_hbm, xe_hbm, cot_hbm, seg_ref, w_hbm, vec_ref, act_hbm, g1_hbm, gr_hbm, g1e_hbm, g_hbm, vg_hbm,
-    w_ref, x_ref, cot_ref, q_ref, k_ref, v_ref, o_ref, p_ref, bias_ref, acc_ref, n2_ref, a2_ref, rs2_ref,
-    g2_ref, a1_ref, a3_ref, gu_ref, vg_ref, bup_ref, sem,
+    x_hbm, cot_hbm, seg_ref, qkv_hbm, out_hbm, up_hbm, vec_hbm, down_hbm,
+    act_hbm, gx_hbm, fin_hbm, find_hbm, vg_hbm,
+    w_ref, d_ref, vecs_ref, vec_ref, x_ref, cot_ref, q_ref, k_ref, v_ref, o_ref, p_ref, bias_ref,
+    acc_ref, n2_ref, a2_ref, rs2_ref, g2_ref, a1_ref, gu_ref, vg_ref, bup_ref,
+    ring0, ring1, ring2, ring3, ring4, ring5, ring6, ring7, fin_ref, find_ref, vr_ref,
+    ag_send, ag_recv, ag_local, rs_send, rs_recv, v_send, v_recv, x_send, x_recv, sem,
 ):
-    mine = lax.axis_index("ctx")
-    for i, (src, dst) in enumerate(
-        ((x_hbm, x_ref.at[0:1024]), (xe_hbm, x_ref.at[1024:1536]), (cot_hbm, cot_ref), (w_hbm, w_ref))
-    ):
-        pltpu.make_async_copy(src, dst, sem.at[i]).start()
-    for i, (src, dst) in enumerate(
-        ((x_hbm, x_ref.at[0:1024]), (xe_hbm, x_ref.at[1024:1536]), (cot_hbm, cot_ref), (w_hbm, w_ref))
-    ):
-        pltpu.make_async_copy(src, dst, sem.at[i]).wait()
+    place = Place()
+    mine = place.c
+    a3_ref = x_ref.at[0:1024]
+    gather = Gather(
+        place, (qkv_hbm, out_hbm, up_hbm, vec_hbm, down_hbm), w_ref, d_ref, vecs_ref, ag_send, ag_recv, ag_local
+    )
+    scatter = Scatter(
+        place, w_ref, d_ref, (ring0, ring1, ring2, ring3, ring4, ring5, ring6, ring7), fin_ref, find_ref, rs_send, rs_recv
+    )
+    barrier = pltpu.get_barrier_semaphore()
+    for device in (place.sibling, place.beside, place.across, place.along(1), place.along(2), place.along(3)):
+        pl.semaphore_signal(barrier, 1, device_id=device, device_id_type=MESH)
+    load_x = pltpu.make_async_copy(x_hbm, x_ref.at[0:1024], sem.at[0])
+    load_cot = pltpu.make_async_copy(cot_hbm, cot_ref, sem.at[1])
+    load_x.start()
+    load_cot.start()
+    pl.semaphore_wait(barrier, 6)
+
+    def rows_out(micro):
+        return pl.ds(pl.multiple_of(micro * 512 + mine * BLK, BLK), BLK)
+
+    give = [
+        send(
+            x_hbm.at[rows_out(micro)],
+            x_ref.at[1024 + micro * BLK : 1024 + micro * BLK + BLK],
+            x_send.at[micro],
+            x_recv.at[micro],
+            place.beside,
+        )
+        for micro in range(2)
+    ]
+    gather.start((None, 1))
+    give[0].start()
+    give[1].start()
+    gather.start((2, 0, 3))
+
+    order = [None, 1, 2, 0, 3, 4, ("d", 0), 5, ("d", 1), 6, ("d", 2), 7, ("d", 3)]
+
+    def tick(t):
+        for stage in (5, 4, 3, 2):
+            at = t - (stage - 2)
+            if 0 <= at < len(order):
+                gather.stage(stage, order[at])
 
     def weight(index):
         return w_ref[index].reshape(D, D)
 
+    def weight_down(index):
+        return d_ref[index].reshape(D, D)
+
     def vec(row):
-        return vec_ref[row : row + 1, :].astype(F32)
-
-    vg_ref[...] = jnp.zeros_like(vg_ref)
+        return vec_ref[row : row + 1, :]
 
     def add_vec(row, value):
         vg_ref[row : row + 1, :] += value
+
+    tick(0)
+    gather.start((4, 5, 6, 7))
+    gather.start_down()
+    vg_ref[...] = jnp.zeros_like(vg_ref)
+    attention_masks(seg_ref, bias_ref, mine)
+    tick(1)
+    load_x.wait()
+    tick(2)
+    tick(3)
+    total = vecs_ref[0, 0, 0].astype(F32)
+    for shard in range(1, 16):
+        total = total + vecs_ref[shard // 4, (shard // 2) % 2, shard % 2].astype(F32)
+    vec_ref[...] = total
 
     def first_norm(r):
         rows = pl.ds(r * BLK, BLK)
         normed, _ = norm(x_ref[rows, :].astype(F32))
         a1_ref[rows, :] = (normed * vec(0) + vec(1)).astype(BF16)
 
-    loop(6, first_norm)
-    attention_masks(seg_ref, bias_ref, mine)
+    loop(4, first_norm)
+    give[0].wait_recv()
+    give[1].wait_recv()
+    loop(2, lambda r: first_norm(4 + r))
+    tick(4)
     k_ref[...] = dot(a1_ref[...], weight(1), 1, 0).astype(BF16)
+    tick(5)
     v_ref[...] = (dot(a1_ref[...], weight(2), 1, 0) + vec(3)).astype(BF16)
+    tick(6)
     q_ref[...] = ((dot(a1_ref[0:1024, :], weight(0), 1, 0) + vec(2)).astype(BF16) * 0.125).astype(BF16)
-    loop(12, lambda i: attention_forward(i, (q_ref, k_ref, v_ref, o_ref, p_ref, bias_ref), mine))
+
+    def forward(i):
+        attention_forward(i, (q_ref, k_ref, v_ref, o_ref, p_ref, bias_ref), mine)
+        for t, at in ((7, 3), (8, 7), (9, 11)):
+
+            @pl.when(i == at)
+            def _():
+                tick(t)
+
+    loop(12, forward)
 
     acc_ref[...] = dot(o_ref[...], weight(3), 1, 0)
+    load_cot.wait()
 
     def second_norm(r):
         rows = pl.ds(r * BLK, BLK)
@@ -609,33 +1067,83 @@
         g2_ref[rows, :] = jnp.zeros((BLK, D), F32)
 
     loop(4, second_norm)
+    for j in range(4):
+        bup_ref[j, 0:1] = vec(8 + j)
+        bup_ref[j, 1:2] = jnp.zeros((1, D), F32)
 
     def feed(j):
-        up, down = 4 + j, 8 + j
+        up = 4 + j
         bias = bup_ref[j, 0:1]
 
         def part(r):
             rows = pl.ds(r * 512, 512)
             u = dot(a2_ref[rows, :], weight(up), 1, 0) + bias
-            back = dot(cot_ref[rows, :], weight(down), 1, 1)
+            back = dot(cot_ref[rows, :], weight_down(j), 1, 1)
             square = u * u
             th = jnp.tanh(u * (0.7978845608028654 + 0.035677408136300125 * square))
-            half = 0.5 + 0.5 * th
-            a3_ref[rows, :] = (u * half).astype(BF16)
-            slope = half + (half * (1.0 - th)) * (u * (0.7978845608028654 + 0.10703222440890037 * square))
+            half_up = 0.5 + 0.5 * th
+            a3_ref[rows, :] = (u * half_up).astype(BF16)
+            slope = half_up + (half_up * (1.0 - th)) * (u * (0.7978845608028654 + 0.10703222440890037 * square))
             gu = (back * slope).astype(BF16)
             gu_ref[rows, :] = gu
             bup_ref[j, 1:2] += colsum(gu.astype(F32))
 
         loop(2, part)
-        acc_ref[...] += dot(a3_ref[...], weight(down), 1, 0)
+
+        @pl.when(j < 3)
+        def _():
+            gather.stage(5, 5 + j)
+            gather.stage(4, ("d", j + 1))
+
+        @pl.when(j < 2)
+        def _():
+            gather.stage(3, 6 + j)
+            gather.stage(2, ("d", j + 2))
+
+        @pl.when(j >= 1)
+        def _():
+            scatter.stage(1, 3 + j, (j - 1) % 4)
+            scatter.stage(1, ("d", j - 1), (j - 1) % 2)
+
+        acc_ref[...] += dot(a3_ref[...], weight_down(j), 1, 0)
         g2_ref[...] += dot(gu_ref[...], weight(up), 1, 1)
-        w_ref[down] = dot(a3_ref[...], cot_ref[...], 0, 0).astype(BF16).reshape(4, 4, 48, D)
-        w_ref[up] = dot(a2_ref[...], gu_ref[...], 0, 0).astype(BF16).reshape(4, 4, 48, D)
-
-    for j in range(4):
-        bup_ref[j, 0:1] = vec(8 + j)
-        bup_ref[j, 1:2] = jnp.zeros((1, D), F32)
+
+        @pl.when(j < 3)
+        def _():
+            gather.stage(5, ("d", j + 1))
+
+        @pl.when(j < 2)
+        def _():
+            gather.stage(4, 6 + j)
+            gather.stage(3, ("d", j + 2))
+
+        @pl.when(j < 1)
+        def _():
+            gather.stage(2, 7 + j)
+
+        @pl.when(j >= 1)
+        def _():
+            scatter.stage(2, 3 + j, (j - 1) % 4)
+            scatter.stage(2, ("d", j - 1), (j - 1) % 2)
+
+        gather.stage(6, up)
+        w_ref[up] = dot(a2_ref[...], gu_ref[...], 0, 0).astype(BF16).reshape(4, 2, 2, 48, D)
+        scatter.stage(0, up, j % 4)
+
+        @pl.when(j >= 1)
+        def _():
+            scatter.stage(3, 3 + j, (j - 1) % 4)
+            scatter.stage(3, ("d", j - 1), (j - 1) % 2)
+
+        gather.stage(6, ("d", j))
+        d_ref[j] = dot(a3_ref[...], cot_ref[...], 0, 0).astype(BF16).reshape(2, 2, 192, D)
+        scatter.stage(0, ("d", j), j % 2)
+
+        @pl.when(j >= 1)
+        def _():
+            scatter.stage(4, 3 + j, (j - 1) % 4)
+            scatter.stage(4, ("d", j - 1), (j - 1) % 2)
+
     loop(4, feed)
     for j in range(4):
         vg_ref[8 + j : 9 + j, :] = bup_ref[j, 1:2]
@@ -659,81 +1167,170 @@
     loop(4, second_back)
     out_copy = pltpu.make_async_copy(a3_ref, act_hbm, sem.at[0])
     out_copy.start()
+    last = [(7, 3), (("d", 3), 1)]
+    for block, slot in last:
+        scatter.stage(1, block, slot)
     gu_ref[...] = dot(a2_ref[...], weight(3), 1, 1).astype(BF16)
-    w_ref[3] = dot(o_ref[...], a2_ref[...], 0, 0).astype(BF16).reshape(4, 4, 48, D)
-    loop(12, lambda i: attention_backward(i, (q_ref, k_ref, v_ref, gu_ref, p_ref), mine))
+    gather.stage(6, 3)
+    w_ref[3] = dot(o_ref[...], a2_ref[...], 0, 0).astype(BF16).reshape(4, 2, 2, 48, D)
+    scatter.stage(0, 3, 0)
+    for block, slot in last:
+        scatter.stage(2, block, slot)
+
+    def backward(i):
+        attention_backward(i, (q_ref, k_ref, v_ref, gu_ref, p_ref), mine)
+
+        @pl.when(i == 2)
+        def _():
+            scatter.stage(1, 3, 0)
+            for block, slot in last:
+                scatter.stage(3, block, slot)
+
+        @pl.when(i == 5)
+        def _():
+            out_copy.wait()
+            load_x.start()
+            scatter.stage(2, 3, 0)
+            for block, slot in last:
+                scatter.stage(4, block, slot)
+
+        @pl.when(i == 8)
+        def _():
+            scatter.stage(3, 3, 0)
+
+        @pl.when(i == 11)
+        def _():
+            scatter.stage(4, 3, 0)
+
+    loop(12, backward)
+
+    gather.stage(6, 0)
+    gather.stage(6, 1)
+    gather.stage(6, 2)
+    a2_ref[0:512, :] = (
+        dot(k_ref[1024:1536, :], weight(1), 1, 1) + dot(v_ref[1024:1536, :], weight(2), 1, 1)
+    ).astype(BF16)
+    give_back = send(a2_ref.at[0:512], bias_ref, x_send.at[2], x_recv.at[2], place.beside)
+    give_back.start()
+    acc_ref[...] = dot(v_ref[0:1024, :], weight(2), 1, 1)
+    w_ref[2] = dot(a1_ref[...], v_ref[...], 0, 0).astype(BF16).reshape(4, 2, 2, 48, D)
+    scatter.stage(0, 2, 1)
+    acc_ref[...] += dot(k_ref[0:1024, :], weight(1), 1, 1)
+    w_ref[1] = dot(a1_ref[...], k_ref[...], 0, 0).astype(BF16).reshape(4, 2, 2, 48, D)
+    scatter.stage(1, 2, 1)
+    scatter.stage(0, 1, 2)
+    acc_ref[...] += dot(q_ref[...], weight(0), 1, 1)
+    w_ref[0] = dot(a1_ref[0:1024, :], q_ref[...], 0, 0).astype(BF16).reshape(4, 2, 2, 48, D)
+    scatter.stage(2, 2, 1)
+    scatter.stage(1, 1, 2)
+    scatter.stage(0, 0, 3)
 
     add_vec(2, colsum(q_ref[...].astype(F32)))
     add_vec(3, colsum(v_ref[...].astype(F32)))
-    out_copy.wait()
-    g1e = dot(k_ref[1024:1536, :], weight(1), 1, 1) + dot(v_ref[1024:1536, :], weight(2), 1, 1)
-    a3_ref[0:512, :] = g1e.astype(BF16)
-    acc_ref[...] = dot(q_ref[...], weight(0), 1, 1)
-    acc_ref[...] += dot(k_ref[0:1024, :], weight(1), 1, 1)
-    acc_ref[...] += dot(v_ref[0:1024, :], weight(2), 1, 1)
-    w_ref[0] = dot(a1_ref[0:1024, :], q_ref[...], 0, 0).astype(BF16).reshape(4, 4, 48, D)
-    w_ref[1] = dot(a1_ref[...], k_ref[...], 0, 0).astype(BF16).reshape(4, 4, 48, D)
-    w_ref[2] = dot(a1_ref[...], v_ref[...], 0, 0).astype(BF16).reshape(4, 4, 48, D)
 
     def extra_back(r):
         rows = pl.ds(1024 + r * BLK, BLK)
         normed, _ = norm(x_ref[rows, :].astype(F32))
-        g1 = a3_ref[pl.ds(r * BLK, BLK), :].astype(F32)
+        g1 = a2_ref[pl.ds(r * BLK, BLK), :].astype(F32)
         add_vec(0, colsum(g1 * normed))
         add_vec(1, colsum(g1))
 
     loop(2, extra_back)
 
-    def first_back(r):
+    def first_sums(r):
         rows = pl.ds(r * BLK, BLK)
         normed, inverse = norm(x_ref[rows, :].astype(F32))
         g1 = acc_ref[rows, :]
         add_vec(0, colsum(g1 * normed))
         add_vec(1, colsum(g1))
 
+    load_x.wait()
+    loop(4, first_sums)
+    def exchange(index, slot, device):
+        return send(vg_ref, vr_ref.at[slot], v_send.at[index], v_recv.at[index], device)
+
+    def add_up(indices):
+        for index, device in indices:
+            exchange(index, index, device).start()
+        for index, device in indices:
+            exchange(index, index, device).wait()
+        value = vg_ref[...]
+        for index, device in indices:
+            value = value + vr_ref[index]
+        vg_ref[...] = value
+
+    add_up([(0, place.sibling)])
+    scatter.stage(3, 2, 1)
+    scatter.stage(2, 1, 2)
+    scatter.stage(1, 0, 3)
+    give_back.wait_recv()
+
+    def first_back(r):
+        rows = pl.ds(r * BLK, BLK)
+        normed, inverse = norm(x_ref[rows, :].astype(F32))
+        t = acc_ref[rows, :] * vec(0)
+        first = jnp.mean(t, -1, keepdims=True)
+        second = jnp.mean(t * normed, -1, keepdims=True)
+        gu_ref[rows, :] = (g2_ref[rows, :] + inverse * (t - first - normed * second)).astype(BF16)
+
+    for micro in range(2):
+        acc_ref[rows_out(micro), :] += bias_ref[micro * BLK : micro * BLK + BLK, :].astype(F32)
     loop(4, first_back)
-    pairs = ((acc_ref, g1_hbm), (g2_ref, gr_hbm), (a3_ref.at[0:512], g1e_hbm), (w_ref, g_hbm), (vg_ref, vg_hbm))
-    for i, (src, dst) in enumerate(pairs):
-        pltpu.make_async_copy(src, dst, sem.at[i]).start()
-    for i, (src, dst) in enumerate(pairs):
-        pltpu.make_async_copy(src, dst, sem.at[i]).wait()
+    gx_copy = pltpu.make_async_copy(gu_ref, gx_hbm, sem.at[1])
+    gx_copy.start()
+    add_up([(1, place.beside)])
+    scatter.stage(4, 2, 1)
+    scatter.stage(3, 1, 2)
+    scatter.stage(2, 0, 3)
+    add_up([(2, place.across)])
+    scatter.stage(4, 1, 2)
+    scatter.stage(3, 0, 3)
+    add_up([(3, place.along(1)), (4, place.along(2)), (5, place.along(3))])
+    scatter.stage(4, 0, 3)
+    blocks = [(4 + j, j) for j in range(4)] + [(("d", j), j % 2) for j in range(4)] + [(3, 0), (2, 1), (1, 2), (0, 3)]
+    for block, slot in blocks:
+        scatter.stage(5, block, slot)
+    ends = [
+        pltpu.make_async_copy(source, target, sem.at[2 + i])
+        for i, (source, target) in enumerate(((fin_ref, fin_hbm), (find_ref, find_hbm), (vg_ref, vg_hbm)))
+    ]
+    for copy in ends:
+        copy.start()
+    for block, slot in blocks:
+        scatter.finish(block, slot)
+    gather.stage(6, None)
+    gather.finish()
+    give[0].wait_send()
+    give[1].wait_send()
+    give_back.wait_send()
+    gx_copy.wait()
+    for copy in ends:
+        copy.wait()
 
 
 def fast_device(
     layer_input, segments, ln1_gain, ln1_bias, w_qkv, q_bias, v_bias, w_attn_out, b_attn_out,
     ln2_gain, ln2_bias, w_up, b_up, w_down, b_down, cotangent,
 ):
-    mine = lax.axis_index("ctx")
-    x = layer_input.reshape(1024, D)
-    cot = cotangent.reshape(1024, D)
-    seg = segments.reshape(2, 1024)
-    own = lax.dynamic_slice_in_dim(x.reshape(2, 512, D), mine * BLK, BLK, 1)
-    extra = lax.ppermute(own, "ctx", ((0, 1), (1, 0))).reshape(512, D)
-
-    def gather(v):
-        return lax.all_gather(v, "fsdp", axis=0, tiled=True)
-
-    qkv, up = gather(w_qkv), gather(w_up)
-    blocks = [qkv[:, D * i : D * i + D] for i in range(3)] + [gather(w_attn_out)]
-    blocks += [up[:, D * i : D * i + D] for i in range(4)]
-    w = jnp.concatenate([jnp.stack(blocks), gather(w_down).reshape(4, D, D)]).reshape(12, 4, 4, 48, D)
-    rows = [ln1_gain, ln1_bias, q_bias, v_bias, b_attn_out, ln2_gain, ln2_bias, b_down]
-    vec = jnp.concatenate(
-        [jnp.stack([gather(v) for v in rows]), gather(b_up).reshape(4, D), jnp.zeros((4, D), BF16)]
-    )
+    f = lax.axis_index("fsdp")
+    rows = jnp.stack([ln1_gain, ln1_bias, q_bias, v_bias, b_attn_out, ln2_gain, ln2_bias, b_down])
+    vec = lax.dynamic_update_slice(jnp.zeros((16, D), BF16), rows, (0, f * 48))
+    vec = lax.dynamic_update_slice(vec, b_up[None], (8 + f // 4, (f % 4) * 192))
     big = lambda *shape, dtype=BF16: jax.ShapeDtypeStruct(shape, dtype)
     hbm = pl.BlockSpec(memory_space=pltpu.HBM)
     vmem = pl.BlockSpec(memory_space=pltpu.VMEM)
-    act, g1, gr, g1e, g, vg = pl.pallas_call(
+    act, gx, fin, find, sums = pl.pallas_call(
         layer_kernel,
         out_shape=(
-            big(1024, D), big(1024, D, dtype=F32), big(1024, D, dtype=F32), big(512, D),
-            big(12, 4, 4, 48, D), big(16, D, dtype=F32),
+            big(1024, D), big(1024, D), big(8, 48, D), big(192, D), big(16, D, dtype=F32),
         ),
-        in_specs=[hbm, hbm, hbm, vmem, hbm, vmem],
-        out_specs=(hbm,) * 6,
+        in_specs=[hbm, hbm, vmem, hbm, hbm, hbm, hbm, hbm],
+        out_specs=(hbm,) * 5,
         scratch_shapes=[
-            pltpu.VMEM((12, 4, 4, 48, D), BF16),
+            pltpu.VMEM((8, 4, 2, 2, 48, D), BF16),
+            pltpu.VMEM((4, 2, 2, 192, D), BF16),
+            pltpu.VMEM((4, 2, 2, 16, D), BF16),
+            pltpu.VMEM((16, D), F32),
             pltpu.VMEM((1536, D), BF16),
             pltpu.VMEM((1024, D), BF16),
             pltpu.VMEM((1024, D), BF16),
@@ -741,7 +1338,7 @@
             pltpu.VMEM((1536, D), BF16),
             pltpu.VMEM((1024, D), BF16),
             pltpu.VMEM((12, 2, 3 * BLK, BLK), BF16),
-            pltpu.VMEM((2, 3 * BLK, BLK), F32),
+            pltpu.VMEM((2 * BLK, 3 * BLK), BF16),
             pltpu.VMEM((1024, D), F32),
             pltpu.VMEM((1024, D), BF16),
             pltpu.VMEM((1024, D), BF16),
@@ -749,36 +1346,45 @@
             pltpu.VMEM((1024, D), F32),
             pltpu.VMEM((1536, D), BF16),
             pltpu.VMEM((1024, D), BF16),
-            pltpu.VMEM((1024, D), BF16),
             pltpu.VMEM((16, D), F32),
             pltpu.VMEM((4, 8, D), F32),
-            pltpu.SemaphoreType.DMA((8,)),
+            pltpu.VMEM((4, 4, 2, 48, D), BF16),
+            pltpu.VMEM((2, 2, 192, D), BF16),
+            pltpu.VMEM((4, 4, 2, 48, HALF), BF16),
+            pltpu.VMEM((2, 2, 192, HALF), BF16),
+            pltpu.VMEM((4, 4, 48, HALF), BF16),
+            pltpu.VMEM((2, 192, HALF), BF16),
+            pltpu.VMEM((4, 3, 48, HALF), BF16),
+            pltpu.VMEM((3, 192, HALF), BF16),
+            pltpu.VMEM((8, 48, D), BF16),
+            pltpu.VMEM((192, D), BF16),
+            pltpu.VMEM((6, 16, D), F32),
+            pltpu.SemaphoreType.DMA((14, 9)),
+            pltpu.SemaphoreType.DMA((14, 9)),
+            pltpu.SemaphoreType.DMA((13,)),
+            pltpu.SemaphoreType.DMA((12, 8)),
+            pltpu.SemaphoreType.DMA((12, 8)),
+            pltpu.SemaphoreType.DMA((6,)),
+            pltpu.SemaphoreType.DMA((6,)),
+            pltpu.SemaphoreType.DMA((3,)),
+            pltpu.SemaphoreType.DMA((3,)),
+            pltpu.SemaphoreType.DMA((5,)),
         ],
-        compiler_params=pltpu.CompilerParams(vmem_limit_bytes=63_000_000),
+        compiler_params=pltpu.CompilerParams(
+            vmem_limit_bytes=66_500_000, collective_id=0, has_side_effects=True
+        ),
         name="layer",
-    )(x, extra, cot, seg, w, vec)
-    back = lax.ppermute(g1e.astype(F32), "ctx", ((0, 1), (1, 0))).reshape(2, BLK, D)
-    g1 = g1.reshape(2, 512, D)
-    mid = lax.dynamic_slice_in_dim(g1, mine * BLK, BLK, 1) + back
-    g1 = lax.dynamic_update_slice_in_dim(g1, mid, mine * BLK, 1).reshape(1024, D)
-    normed, inverse = normalize_parts(x.astype(F32))
-    gx = (gr + normalize_back(g1 * vec[0].astype(F32), normed, inverse)).astype(BF16)
-    g = g.astype(F32).reshape(12, D, D)
-
-    def scatter(v):
-        return lax.psum(lax.psum_scatter(v, "fsdp", scatter_dimension=0, tiled=True), "ctx")
-
-    g_qkv = scatter(jnp.concatenate([g[0], g[1], g[2]], 1))
-    g_out = scatter(g[3])
-    g_up = scatter(jnp.concatenate([g[4], g[5], g[6], g[7]], 1))
-    g_down = scatter(g[8:].reshape(4 * D, D))
-    sums = lax.psum(vg, ("ctx", "fsdp"))
-    f = lax.axis_index("fsdp")
-    part = lambda i: lax.dynamic_slice_in_dim(sums[i], f * 48, 48)
-    g_bup = lax.dynamic_slice_in_dim(sums[8:12].reshape(4 * D), f * 192, 192)
+    )(
+        layer_input.reshape(1024, D), cotangent.reshape(1024, D), segments.reshape(2, 1024),
+        w_qkv, w_attn_out, w_up, vec, w_down,
+    )
+    fin = fin.astype(F32)
+    part = lax.dynamic_slice(sums, (0, f * 48), (8, 48))
+    g_bup = lax.dynamic_slice(sums, (8 + f // 4, (f % 4) * 192), (1, 192))[0]
     return (
-        act.reshape(2, 1, 512, D), gx.reshape(2, 1, 512, D), part(0), part(1), g_qkv, part(2), part(3),
-        g_out, part(4), part(5), part(6), g_up, g_bup, g_down, part(7),
+        act.reshape(2, 1, 512, D), gx.reshape(2, 1, 512, D), part[0], part[1],
+        jnp.concatenate([fin[0], fin[1], fin[2]], 1), part[2], part[3], fin[3], part[4], part[5], part[6],
+        jnp.concatenate([fin[4], fin[5], fin[6], fin[7]], 1), g_bup, find.astype(F32), part[7],
     )
 
 

time: 796 us -> 271 us (0.34); the launches traced: 787 us -> 270 us
  waiting for transfers between devices: 449 us -> 0 us
  Pallas kernels: 105 us -> 256 us
  blocking collectives: 129 us -> 0 us
  local copies, waits for them, and re-layouts: 60.4 us -> 10.4 us
  other arithmetic: 23.9 us -> 3.65 us
  between operations: 15.8 us -> 0.7 us
    reduce_scatter x4 -> x0, waiting for transfers between devices: 294 us -> none  [scatter(): lax.psum_scatter(v, 'fsdp', scatter_dimension=0, tiled=True)]
    pallas_call x1, Pallas kernels: 105 us -> 256 us  [fast_device(): pl.pallas_call(layer_kernel, out_shape=(big(1024, D), big(1024, D), big(8...]
    all_gather x4 -> x0, waiting for transfers between devices: 105 us -> none  [gather(): return lax.all_gather(v, 'fsdp', axis=0, tiled=True)]
    psum x1 -> x0, blocking collectives: 67 us -> none  [fast_device(): sums = lax.psum(vg, ('ctx', 'fsdp'))]
    unnamed x1 -> x0, blocking collectives: 61.7 us -> none
    psum x1 -> x0, waiting for transfers between devices: 46.7 us -> none  [scatter(): lax.psum(lax.psum_scatter(v, 'fsdp', scatter_dimension=0, tiled=True), 'c...]
    unnamed x48 -> x11, local copies, waits for them, and re-layouts: 29.4 us -> 5.03 us
    slice x6 -> x0, local copies, waits for them, and re-layouts: 20.5 us -> none  [the longest x1 8.24 us: fast_device(): g_up = scatter(jnp.concatenate([g[4], g[5], g[6], g[7]], 1))]
  transfers between devices with their start and end apart: 11 -> 0, of which waited for: 7 -> 0; matrix products, arithmetic and copies ran while one was open for 9% -> 0% of each run, Pallas kernels for 0% -> 0%
where the time goes in v2:
time: 271 us; the launch traced here: 270 us
  Pallas kernels  256 us (94%)
  local copies, waits for them, and re-layouts  10.4 us (4%)
  other arithmetic  3.65 us (1%)
    pallas_call x1, Pallas kernels, fast_device(): pl.pallas_call(layer_kernel, out_shape=(big(1024, D), big(1024, D), big(8...  256 us

profile of v2, /device:TPU:0, one launch (start us, length us, event | category | flops | bytes accessed | tf_op | source)
XLA Modules:
  0.0 270.4 jit_solution(6406389913584221638)
XLA Ops:
  0.6 1.3 copy.35
  1.9 0.8 stack.35
  2.8 0.3 dynamic_update_slice.6
  3.1 0.7 broadcast_in_dim.7
  3.7 0.1 dynamic_update_slice.7.vec_hbm
  3.9 0.0 copy-start.3
  3.9 0.6 copy-done.3
  4.5 255.7 %layer.1 = (bf16[1024,768]{1,0:T(8,128)(2,1)}, bf16[1024,768]{1,0:T(8,128)(2,1)}, bf16[8,48,768]{2,1,0:T(8,128)(2,1)}, bf16[192,768]{1,0:T(8,128)(2,1)}, f32[16,768]{1,0:T(8,128)}) custom-call(bf16[1024,768]{1,0:T(8,128)(2,1)} %bitcast.54, bf16[1024,768]{1,0:T(8,128)(2,1)} %bitcast.55, s32[2,1024]{1,0:T(2,128)} %bitcast.56, bf16[48,2304]{1,0:T(8,128)(2,1)} %qkv_hbm.1, ...), custom_call_target="tpu_custom_call" | custom-call | tf_op jit(solution)/shard_map/layer/pallas_call | solution.py:1322
  260.2 0.8 constant_dynamic-slice_fusion
  261.0 0.5 slice_bitcast_fusion.8
  261.5 1.2 convert_element_type.6
  262.7 0.8 slice_bitcast_fusion.3
  263.5 0.0 copy-start.2
  263.5 0.0 copy-start.1
  263.5 0.8 pad_maximum_fusion.1
  264.2 0.9 pad_maximum_fusion
  265.1 1.3 dynamic_slice.7
  266.4 0.0 copy-done.2
  266.4 0.9 convert_element_type.7
  267.3 0.0 copy-done.1
  267.3 0.0 copy-start
  267.3 1.1 copy.40
  268.5 0.8 copy-done
  269.3 1.1 copy.41
  (1 shorter events, 0.0 us)
Async XLA Ops:
  3.9 0.6 copy-start.3
  263.5 3.0 %copy-start.2 = (bf16[192,768]{1,0:T(8,128)(2,1)S(1)}, bf16[192,768]{1,0:T(8,128)(2,1)}, u32[]{:S(2)}) copy-start(bf16[192,768]{1,0:T(8,128)(2,1)} %get-tuple-element.24) | copy-start | bytes 884740
  263.5 3.8 %copy-start.1 = (bf16[1024,768]{1,0:T(8,128)(2,1)S(1)}, bf16[1024,768]{1,0:T(8,128)(2,1)}, u32[]{:S(2)}) copy-start(bf16[1024,768]{1,0:T(8,128)(2,1)} %get-tuple-element.20) | copy-start | bytes 4718596
  267.3 2.0 copy-start
